TPU v7x, 32 devices: a whole 2x2x4 slice. The times are simulated.
32 devices in a mesh: img: 8 (over y, x, core), strip: 4 (over z).
Axes of the slice: x: 2, y: 2, z: 4, core: 2. Of those that a mesh axis runs over, the one named last changes fastest.
Arguments:
- patches: bfloat16 [64, 576, 300], P('img', 'strip'), may hold values from -6 to 6
- pinv: float32 [100, 1024], replicated, may hold values from -0.1875 to 0.1875
- base_embed: float32 [3, 1024, 384], replicated, may hold values from -0.375 to 0.375
- bias_embed: float32 [384], replicated, may hold values from -2 to 2
- pos_grid: float32 [7, 7, 384], replicated, may hold values from -6 to 6
- pos_index: int32 [2, 2, 24], replicated, may hold values from 0 to 6
- pos_frac: float32 [2, 24], replicated, may hold values from 0 to 1
- norm_gain: float32 [2, 384], replicated, may hold values from 0.5 to 1.5
- norm_shift: float32 [2, 384], replicated, may hold values from -2 to 2
- w_qkv: bfloat16 [384, 1152], replicated, may hold values from -0.3125 to 0.3125
- bias_attn: float32 [3, 384], replicated, may hold values from -2 to 2
- w_out: bfloat16 [384, 384], replicated, may hold values from -4 to 4
- w_up: bfloat16 [384, 1536], replicated, may hold values from -0.3125 to 0.3125
- bias_up: float32 [1536], replicated, may hold values from -2 to 2
- w_down: bfloat16 [1536, 384], replicated, may hold values from -0.15625 to 0.15625
- bias_down: float32 [384], replicated, may hold values from -2 to 2
- cotangent: bfloat16 [64, 576, 384], P('img', 'strip'), may hold values from -6 to 6
Outputs:
- output: bfloat16 [64, 576, 384], P('img', 'strip')
- g_patches: bfloat16 [64, 576, 300], P('img', 'strip')
- g_base_embed: float32 [3, 1024, 384], replicated
- g_bias_embed: float32 [384], replicated
- g_pos_grid: float32 [7, 7, 384], replicated
- g_norm_gain: float32 [2, 384], replicated
- g_norm_shift: float32 [2, 384], replicated
- g_w_qkv: float32 [384, 1152], replicated
- g_bias_attn: float32 [3, 384], replicated
- g_w_out: float32 [384, 384], replicated
- g_w_up: float32 [384, 1536], replicated
- g_bias_up: float32 [1536], replicated
- g_w_down: float32 [1536, 384], replicated
- g_bias_down: float32 [384], replicated
Inputs may be any that keep to these rules, and one draw needn't show every extreme that they name: `pos_index`: each entry names a row or column of the base positional grid.
All inputs are finite; a program needn't handle non-finite values.
Results may differ from a plain program's by a relative error of at most 0.015.
Values may be sent and summed in bfloat16 or wider, within the bound.
A program may use at most 192 MiB of HBM per device.

v0:
```python
from functools import partial
import math

import jax
import jax.numpy as jnp
from jax import lax
from jax.sharding import PartitionSpec as P

HD = 64


HIGHEST = lax.Precision.HIGHEST
EPSILON = 1e-06


def resize_table(corner_index, fraction, base_count):
    base_cells = jnp.arange(base_count, dtype=jnp.int32)
    lower_hit = (corner_index[0][:, None] == base_cells[None, :]).astype(jnp.float32)
    upper_hit = (corner_index[1][:, None] == base_cells[None, :]).astype(jnp.float32)
    return (1.0 - fraction)[:, None] * lower_hit + fraction[:, None] * upper_hit


def norm_parts(values_in, gain_row, shift_row):
    center = values_in - jnp.mean(values_in, axis=-1, keepdims=True)
    inv_std = lax.rsqrt(jnp.mean(center * center, axis=-1, keepdims=True) + EPSILON)
    unit_rows = center * inv_std
    return (unit_rows * gain_row + shift_row, unit_rows, inv_std)


def norm_back(gradient, unit_rows, inv_std, gain_row):
    g_unit = gradient * gain_row
    g_gain = jnp.sum(gradient * unit_rows, axis=(0, 1))
    g_shift = jnp.sum(gradient, axis=(0, 1))
    g_input = inv_std * (
        g_unit
        - jnp.mean(g_unit, axis=-1, keepdims=True)
        - unit_rows * jnp.mean(g_unit * unit_rows, axis=-1, keepdims=True)
    )
    return (g_input, g_gain, g_shift)


def split_heads(values_in, head_count):
    return values_in.reshape(
        values_in.shape[0], values_in.shape[1], head_count, values_in.shape[2] // head_count
    )


def score_block(queries, keys_all, head_count):
    factor = 1.0 / math.sqrt(queries.shape[2] // head_count)
    return (
        jnp.einsum(
            "iqhe,ikhe->ihqk",
            split_heads(queries, head_count),
            split_heads(keys_all, head_count),
            preferred_element_type=jnp.float32,
        )
        * factor
    )


def per_device(
    patches,
    pinv,
    base_embed,
    bias_embed,
    pos_grid,
    pos_index,
    pos_frac,
    norm_gain,
    norm_shift,
    w_qkv,
    bias_attn,
    w_out,
    w_up,
    bias_up,
    w_down,
    bias_down,
    cotangent,
):
    images, rows_dev, pixels = patches.shape
    model_width = w_qkv.shape[0]
    head_count = model_width // HD
    factor = 1.0 / math.sqrt(HD)
    grid_side = pos_frac.shape[1]
    strip_rows = rows_dev // grid_side
    base_count = pos_grid.shape[0]
    first_row = lax.axis_index("strip") * strip_rows
    row_table = resize_table(pos_index[0], pos_frac[0], base_count)
    row_local = lax.dynamic_slice_in_dim(row_table, first_row, strip_rows, 0)
    col_table = resize_table(pos_index[1], pos_frac[1], base_count)
    position = jnp.einsum(
        "rb,cg,bgd->rcd", row_local, col_table, pos_grid, precision=HIGHEST
    ).reshape(rows_dev, model_width)
    kernel = (
        jnp.einsum("qk,ckd->cqd", pinv, base_embed, precision=HIGHEST)
        .reshape(pixels, model_width)
        .astype(jnp.bfloat16)
    )
    embedded = (
        jnp.einsum("isp,pd->isd", patches, kernel, preferred_element_type=jnp.float32)
        + bias_embed
        + position
    )
    normed, unit_one, inv_one = norm_parts(embedded, norm_gain[0], norm_shift[0])
    normed = normed.astype(jnp.bfloat16)
    projected = jnp.einsum("isd,de->ise", normed, w_qkv, preferred_element_type=jnp.float32)
    queries = (projected[:, :, :model_width] + bias_attn[0]).astype(jnp.bfloat16)
    keys_local = projected[:, :, model_width : 2 * model_width].astype(jnp.bfloat16)
    values_local = (projected[:, :, 2 * model_width :] + bias_attn[1]).astype(jnp.bfloat16)
    keys_all, values_all = (
        lax.all_gather(keys_local, "strip", axis=1, tiled=True),
        lax.all_gather(values_local, "strip", axis=1, tiled=True),
    )
    scores = score_block(queries, keys_all, head_count)
    row_max = jnp.max(scores, axis=-1, keepdims=True)
    expo = jnp.exp(scores - row_max)
    row_total = jnp.sum(expo, axis=-1, keepdims=True)
    log_total = row_max + jnp.log(row_total)
    probs_low = (expo / row_total).astype(jnp.bfloat16)
    attended = jnp.einsum(
        "ihqk,ikhe->iqhe",
        probs_low,
        split_heads(values_all, head_count),
        preferred_element_type=jnp.float32,
    )
    attended = attended.reshape(images, rows_dev, model_width).astype(jnp.bfloat16)
    middle = (
        embedded
        + jnp.einsum("isd,de->ise", attended, w_out, preferred_element_type=jnp.float32)
        + bias_attn[2]
    )
    normed_mlp, unit_two, inv_two = norm_parts(middle, norm_gain[1], norm_shift[1])
    normed_mlp = normed_mlp.astype(jnp.bfloat16)
    up_proj = (
        jnp.einsum("isd,df->isf", normed_mlp, w_up, preferred_element_type=jnp.float32) + bias_up
    )
    gelu_fn = partial(jax.nn.gelu, approximate=True)
    activated = gelu_fn(up_proj).astype(jnp.bfloat16)
    output = (
        middle
        + jnp.einsum("isf,fd->isd", activated, w_down, preferred_element_type=jnp.float32)
        + bias_down
    )
    grad_out = cotangent.astype(jnp.float32)
    g_bias_down = jnp.sum(grad_out, axis=(0, 1))
    g_w_down = jnp.einsum("isf,isd->fd", activated, cotangent, preferred_element_type=jnp.float32)
    g_activated = jnp.einsum("isd,fd->isf", cotangent, w_down, preferred_element_type=jnp.float32)
    g_up = jax.vjp(gelu_fn, up_proj)[1](g_activated)[0].astype(jnp.bfloat16)
    g_bias_up = jnp.sum(g_up.astype(jnp.float32), axis=(0, 1))
    g_w_up = jnp.einsum("isd,isf->df", normed_mlp, g_up, preferred_element_type=jnp.float32)
    g_normed_mlp = jnp.einsum("isf,df->isd", g_up, w_up, preferred_element_type=jnp.float32)
    g_middle_norm, g_gain_two, g_shift_two = norm_back(
        g_normed_mlp, unit_two, inv_two, norm_gain[1]
    )
    g_middle = grad_out + g_middle_norm
    g_branch = g_middle.astype(jnp.bfloat16)
    g_bias_out = jnp.sum(g_branch.astype(jnp.float32), axis=(0, 1))
    g_w_out = jnp.einsum("isd,ise->de", attended, g_branch, preferred_element_type=jnp.float32)
    g_attended = jnp.einsum(
        "ise,de->isd", g_branch, w_out, preferred_element_type=jnp.float32
    ).astype(jnp.bfloat16)
    keys_back, values_back = (keys_all, values_all)
    probs_back = jnp.exp(score_block(queries, keys_back, head_count) - log_total)
    g_attended4 = split_heads(g_attended, head_count)
    g_probs = jnp.einsum(
        "iqhe,ikhe->ihqk",
        g_attended4,
        split_heads(values_back, head_count),
        preferred_element_type=jnp.float32,
    )
    row_delta = jnp.sum(probs_back * g_probs, axis=-1, keepdims=True)
    g_scores = (probs_back * (g_probs - row_delta)).astype(jnp.bfloat16)
    g_queries = factor * jnp.einsum(
        "ihqk,ikhe->iqhe",
        g_scores,
        split_heads(keys_back, head_count),
        preferred_element_type=jnp.float32,
    )
    g_keys_all = factor * jnp.einsum(
        "ihqk,iqhe->ikhe",
        g_scores,
        split_heads(queries, head_count),
        preferred_element_type=jnp.float32,
    )
    g_values_all = jnp.einsum(
        "ihqk,iqhe->ikhe",
        probs_back.astype(jnp.bfloat16),
        g_attended4,
        preferred_element_type=jnp.float32,
    )
    seq_all = keys_back.shape[1]
    g_keys, g_values = (
        lax.psum_scatter(
            g_keys_all.reshape(images, seq_all, model_width).astype(jnp.bfloat16),
            "strip",
            scatter_dimension=1,
            tiled=True,
        ).astype(jnp.float32),
        lax.psum_scatter(
            g_values_all.reshape(images, seq_all, model_width).astype(jnp.bfloat16),
            "strip",
            scatter_dimension=1,
            tiled=True,
        ).astype(jnp.float32),
    )
    g_projected = jnp.concatenate(
        [g_queries.reshape(images, rows_dev, model_width), g_keys, g_values], axis=-1
    ).astype(jnp.bfloat16)
    g_bias_q = jnp.sum(g_projected[:, :, :model_width].astype(jnp.float32), axis=(0, 1))
    g_bias_v = jnp.sum(g_projected[:, :, 2 * model_width :].astype(jnp.float32), axis=(0, 1))
    g_w_qkv = jnp.einsum("isd,ise->de", normed, g_projected, preferred_element_type=jnp.float32)
    g_normed = jnp.einsum("ise,de->isd", g_projected, w_qkv, preferred_element_type=jnp.float32)
    g_embed_norm, g_gain_one, g_shift_one = norm_back(g_normed, unit_one, inv_one, norm_gain[0])
    g_embedded = (g_middle + g_embed_norm).astype(jnp.bfloat16)
    g_patches = jnp.einsum(
        "isd,pd->isp", g_embedded, kernel, preferred_element_type=jnp.float32
    ).astype(jnp.bfloat16)
    g_kernel = jnp.einsum("isp,isd->pd", patches, g_embedded, preferred_element_type=jnp.float32)
    g_embed_f = g_embedded.astype(jnp.float32)
    g_bias_embed = jnp.sum(g_embed_f, axis=(0, 1))
    g_position = jnp.sum(g_embed_f, axis=0).reshape(strip_rows, grid_side, model_width)
    g_grid = jnp.einsum("rb,cg,rcd->bgd", row_local, col_table, g_position, precision=HIGHEST)
    patch_area = pinv.shape[0]
    kernel_term = jnp.einsum(
        "qk,cqd->ckd", pinv, g_kernel.reshape(3, patch_area, model_width), precision=HIGHEST
    )
    shares = (
        lax.psum_scatter(g_w_qkv.reshape(-1), ("img", "strip"), scatter_dimension=0, tiled=True),
        lax.psum_scatter(g_w_out.reshape(-1), ("img", "strip"), scatter_dimension=0, tiled=True),
        lax.psum_scatter(g_w_up.reshape(-1), ("img", "strip"), scatter_dimension=0, tiled=True),
        lax.psum_scatter(g_w_down.reshape(-1), ("img", "strip"), scatter_dimension=0, tiled=True),
        lax.psum_scatter(
            kernel_term.reshape(-1), ("img", "strip"), scatter_dimension=0, tiled=True
        ),
    )
    gathered = (
        lax.all_gather(shares[0].astype(jnp.bfloat16), ("img", "strip"), axis=0, tiled=True).astype(
            jnp.float32
        ),
        lax.all_gather(shares[1].astype(jnp.bfloat16), ("img", "strip"), axis=0, tiled=True).astype(
            jnp.float32
        ),
        lax.all_gather(shares[2].astype(jnp.bfloat16), ("img", "strip"), axis=0, tiled=True).astype(
            jnp.float32
        ),
        lax.all_gather(shares[3].astype(jnp.bfloat16), ("img", "strip"), axis=0, tiled=True).astype(
            jnp.float32
        ),
        lax.all_gather(shares[4].astype(jnp.bfloat16), ("img", "strip"), axis=0, tiled=True).astype(
            jnp.float32
        ),
    )
    g_base = gathered[4].reshape(base_embed.shape)
    small_grads = lax.psum(
        (
            jnp.stack([g_gain_one, g_gain_two]),
            jnp.stack([g_shift_one, g_shift_two]),
            jnp.stack([g_bias_q, g_bias_v, g_bias_out]),
            g_bias_up,
            g_bias_down,
            g_bias_embed,
            g_grid,
        ),
        ("img", "strip"),
    )
    return (
        output.astype(jnp.bfloat16),
        g_patches,
        g_base,
        small_grads[5],
        small_grads[6],
        small_grads[0],
        small_grads[1],
        gathered[0].reshape(w_qkv.shape),
        small_grads[2],
        gathered[1].reshape(w_out.shape),
        gathered[2].reshape(w_up.shape),
        small_grads[3],
        gathered[3].reshape(w_down.shape),
        small_grads[4],
    )


def solution(mesh):
    in_specs = (
        P("img", "strip", None),
        P(),
        P(),
        P(),
        P(),
        P(),
        P(),
        P(),
        P(),
        P(),
        P(),
        P(),
        P(),
        P(),
        P(),
        P(),
        P("img", "strip", None),
    )
    out_specs = (
        P("img", "strip", None),
        P("img", "strip", None),
        P(),
        P(),
        P(),
        P(),
        P(),
        P(),
        P(),
        P(),
        P(),
        P(),
        P(),
        P(),
    )
    return jax.shard_map(
        per_device, mesh=mesh, in_specs=in_specs, out_specs=out_specs, check_vma=False
    )
```

profile of v0, /device:TPU:0, one launch (start us, length us, event | category | flops | bytes accessed | tf_op | source)
XLA Modules:
  0.0 792.4 jit_solution(3508578325226030029)
XLA Ops:
  9.6 5.3 fusion.26
  15.8 2.2 fusion.66
  18.7 1.7 fusion.29
  20.4 2.3 copy-done.5
  22.7 1.0 slice.106
  23.9 3.5 fusion.17
  27.7 2.5 copy.77
  30.1 66.5 %all-gather.10.cloned.1.call-done = bf16[8,576,384]{2,1,0:T(8,128)(2,1)} async-done(((bf16[8,144,384]{2,1,0:T(8,128)(2,1)}), bf16[8,576,384]{2,1,0:T(8,128)(2,1)}) %all-gather.10.cloned.1.call-update) | async-done | bytes 3538960 | tf_op jit(solution)/shard_map/all_gather | solution.py:111
  96.6 5.9 copy.78
  102.5 5.9 multiply_reduce_fusion.1
  108.4 4.6 fusion
  113.0 1.5 copy-done.2
  114.5 52.9 %all-gather.8.cloned.1.call-done = bf16[8,576,384]{2,1,0:T(8,128)(2,1)} async-done(((bf16[8,144,384]{2,1,0:T(8,128)(2,1)}), bf16[8,576,384]{2,1,0:T(8,128)(2,1)}) %all-gather.8.cloned.1.call-update) | async-done | bytes 3538960 | tf_op jit(solution)/shard_map/all_gather | solution.py:112
  167.3 5.9 copy.76
  173.2 9.5 %fusion.19 = bf16[8,6,64,144]{3,2,1,0:T(8,128)(2,1)S(1)} fusion(bf16[8,576,6,64]{1,3,2,0:T(8,128)(2,1)} %bitcast.140, f32[8,6,144,576]{3,2,1,0:T(8,128)} %copy-done.2, f32[8,6,144]{2,1,0:T(8,128)S(1)} %fusion, f32[8,6,144]{2,1,0:T(8,128)S(1)} %get-tuple-element.114), kind=kOutput, calls=%fused_computation.56 | convolution fusion | flops 525975552 | bytes 20404224 | tf_op jit(solution)/shard_map/ihqk,ikhe->iqhe/dot_general | solution.py:120
  182.7 1.1 fusion.67
  184.5 4.7 multiply_convert_fusion.2
  189.2 7.3 convert_reduce_fusion
  196.5 2.7 multiply_reduce_fusion.2
  199.2 1.6 convert_reduce_fusion.6
  200.8 1.2 copy-done.8
  202.7 1.6 copy.80
  204.3 9.8 %fusion.14 = bf16[8,6,64,576]{3,2,1,0:T(8,128)(2,1)} fusion(bf16[8,144,6,64]{1,3,2,0:T(8,128)(2,1)} %bitcast.137, f32[8,6,144,576]{3,2,1,0:T(8,128)} %copy-done.2, f32[8,6,144]{2,1,0:T(8,128)S(1)} %log_add_fusion), kind=kOutput, calls=%fused_computation.30 | convolution fusion | flops 523321344 | bytes 20376576 | tf_op jit(solution)/shard_map/ihqk,iqhe->ikhe/dot_general | solution.py:185
  214.1 6.2 copy.82
  220.3 15.2 %multiply_reduce_fusion = (f32[8,6,144]{2,1,0:T(8,128)S(1)}, f32[8,6,144,576]{3,2,1,0:T(8,128)}) fusion(f32[8,6,144,576]{3,2,1,0:T(8,128)} %copy-done.2, f32[8,6,144]{2,1,0:T(8,128)S(1)} %log_add_fusion, bf16[8,144,6,64]{1,3,2,0:T(8,128)(2,1)} %bitcast.138, bf16[8,576,6,64]{1,3,2,0:T(8,128)(2,1)} %bitcast.141), kind=kOutput, calls=%fused_computation.1 | convolution fusion | flops 525526272 | bytes 36329472 | tf_op jit(solution)/shard_map/iqhe,ikhe->ihqk/dot_general | solution.py:165
  235.6 12.7 %multiply_convert_fusion = bf16[8,6,144,576]{3,2,1,0:T(8,128)(2,1)S(1)} fusion(f32[8,6,144,576]{3,2,1,0:T(8,128)} %get-tuple-element.122, f32[8,6,144,576]{3,2,1,0:T(8,128)} %copy-done.2, f32[8,6,144]{2,1,0:T(8,128)S(1)} %get-tuple-element.121, f32[8,6,144]{2,1,0:T(8,128)S(1)} %log_add_fusion), kind=kLoop, calls=%fused_computation | loop fusion | flops 19906560 | bytes 39868416 | tf_op jit(solution)/shard_map/convert_element_type | solution.py:172
  248.3 3.5 multiply_convert_fusion.1
  251.8 1.1 copy-done.3
  252.9 6.2 copy.81
  259.3 0.9 copy-done.18
  260.2 5.6 convolution_bitcast_fusion
  265.8 3.2 reshape.213
  269.0 5.8 convolution_bitcast_fusion.1
  274.8 3.2 reshape.210
  279.1 2.7 convolution_bitcast_fusion.4
  282.4 8.4 %multiply_convert_fusion.3 = bf16[8,6,64,144]{3,2,1,0:T(8,128)(2,1)S(1)} fusion(bf16[8,576,6,64]{1,3,2,0:T(8,128)(2,1)} %bitcast.133, bf16[8,6,144,576]{3,2,1,0:T(8,128)(2,1)} %copy-done.3), kind=kOutput, calls=%fused_computation.25 | convolution fusion | flops 510492672 | bytes 12386304 | tf_op jit(solution)/shard_map/ihqk,ikhe->iqhe/dot_general | solution.py:173
  290.9 1.1 copy-done.9
  292.9 2.8 copy.83
  295.7 1.4 convert_reduce_fusion.7
  297.7 56.6 %reduce-scatter.3.cloned.1.call-done = bf16[8,144,384]{2,1,0:T(8,128)(2,1)} async-done(((bf16[8,576,384]{2,1,0:T(8,128)(2,1)}), bf16[8,144,384]{2,1,0:T(8,128)(2,1)}) %reduce-scatter.3.cloned.1.call-update) | async-done | bytes 884752 | tf_op jit(solution)/shard_map/reduce_scatter | solution.py:193
  354.3 4.8 multiply_reduce_fusion.3
  359.7 2.8 convolution_bitcast_fusion.2
  362.5 2.6 reshape.204
  365.7 3.0 convert_reduce_fusion.2
  370.2 1.8 convolution_bitcast_fusion.5
  372.0 5.5 convolution_bitcast_fusion.3
  377.6 6.0 copy.84
  383.7 5.8 reshape.200
  389.6 200.4 %all-reduce.10 = (bf16[1179648]{0:T(1024)(128)(2,1)}, bf16[589824]{0:T(1024)(128)(2,1)}, bf16[589824]{0:T(1024)(128)(2,1)}, f32[384]{0:T(512)}, f32[2,384]{1,0:T...) all-reduce(f32[1179648]{0:T(1024)} %reshape.200, ...), channel_id=4, replica_groups=mesh['img'=8,'strip'=4] {'img','strip'}, use_global_device_ids=true, to_apply=%region_13.0.clone | all-reduce | flops 2954112 | bytes 17734656
  590.0 1.4 dynamic-slice.12
  591.5 1.4 dynamic-slice.11
  593.0 1.5 dynamic-slice.10
  594.5 5.3 add_convert_fusion.1
  601.5 71.0 %all-gather.1 = bf16[32,1,4608]{2,1,0:T(2,128)(2,1)S(1)} all-gather(bf16[1,1,4608]{2,1,0:T(2,128)(2,1)S(1)} %reshape.228), channel_id=1, replica_groups=mesh['img'=8,'strip'=4] {'img','strip'}, dimensions={0}, use_global_device_ids=true | all-gather | bytes 304128 | tf_op jit(solution)/shard_map/all_gather | solution.py:240
  672.5 1.6 convert_reduce_fusion.8
  674.1 1.0 reshape.221
  675.1 88.5 %all-gather = bf16[32,1,13824]{2,1,0:T(2,128)(2,1)S(1)} all-gather(bf16[1,1,13824]{2,1,0:T(2,128)(2,1)S(1)} %reshape.226), channel_id=1, replica_groups=mesh['img'=8,'strip'=4] {'img','strip'}, dimensions={0}, use_global_device_ids=true | all-gather | bytes 912384 | tf_op jit(solution)/shard_map/all_gather | solution.py:237
  763.6 5.0 convert_reduce_fusion.5
  768.6 1.7 reshape.219
  770.3 1.6 convolution_convert_fusion
  771.9 1.5 copy.87
  773.4 3.5 reshape.223
  776.9 3.2 reshape.225
  780.1 5.0 reshape.217
  (165 shorter events, 13.6 us)
Async XLA Ops:
  7.2 177.3 %copy-start = (bf16[384,1536]{1,0:T(8,128)(2,1)S(1)}, bf16[384,1536]{1,0:T(8,128)(2,1)}, u32[]{:S(2)}) copy-start(bf16[384,1536]{1,0:T(8,128)(2,1)} %param.29) | copy-start | bytes 3538948
  7.2 89.4 %all-gather.10.cloned.1.call-start = ((), (), s32[]{:S(2)}) async-start(), calls=%async_computation.3 | async-start | bytes 4423680 | tf_op jit(solution)/shard_map/all_gather | solution.py:111
  8.0 7.3 copy-start.38
  8.8 6.5 copy-start.40
  9.6 5.8 copy-start.42
  9.6 5.8 copy-start.44
  9.6 5.4 copy-start.21
  9.6 6.2 copy-start.52
  14.9 3.6 copy-start.13
  14.9 0.8 copy-start.22
  15.7 2.8 copy-start.47
  15.8 2.8 copy-start.48
  15.8 2.9 copy-start.15
  18.6 1.8 copy-start.24
  18.6 1.8 copy-start.29
  20.4 2.3 copy-start.5
  22.7 1.1 copy-start.46
  23.8 143.6 %all-gather.8.cloned.1.call-start = ((), (), s32[]{:S(2)}) async-start(), calls=%async_computation.2 | async-start | bytes 4423680 | tf_op jit(solution)/shard_map/all_gather | solution.py:112
  27.4 268.3 %reduce-scatter.5.cloned.1.call-start = ((), (), s32[]{:S(2)}) async-start(), calls=%async_computation.5 | async-start | bytes 4423680 | tf_op jit(solution)/shard_map/reduce_scatter | solution.py:199
  108.4 6.1 copy-start.2
  173.2 9.5 %copy-start.12 = (bf16[384,384]{1,0:T(8,128)(2,1)S(1)}, bf16[384,384]{1,0:T(8,128)(2,1)}, u32[]{:S(2)}) copy-start(bf16[384,384]{1,0:T(8,128)(2,1)} %param.28) | copy-start | bytes 884740
  182.7 1.2 copy-start.11
  182.7 1.7 copy-start.51
  183.9 15.4 %copy-start.6 = (f32[8,144,384]{2,1,0:T(8,128)}, f32[8,144,384]{2,1,0:T(8,128)S(1)}, u32[]{:S(2)}) copy-start(f32[8,144,384]{2,1,0:T(8,128)S(1)} %get-tuple-element.117) | copy-start | bytes 5308420
  184.5 4.7 copy-start.17
  184.5 4.7 copy-start.49
  196.5 2.7 copy-start.54
  200.8 1.2 copy-start.8
  220.3 134.0 %reduce-scatter.3.cloned.1.call-start = ((), (), s32[]{:S(2)}) async-start(), calls=%async_computation.4 | async-start | bytes 4423680 | tf_op jit(solution)/shard_map/reduce_scatter | solution.py:193
  235.6 12.7 %copy-start.4 = (bf16[8,144,384]{1,2,0:T(8,128)(2,1)S(1)}, bf16[8,144,384]{1,2,0:T(8,128)(2,1)}, u32[]{:S(2)}) copy-start(bf16[8,144,384]{1,2,0:T(8,128)(2,1)} %copy.77) | copy-start | bytes 2654212
  248.3 4.6 copy-start.3
  259.1 1.2 copy-start.18
  259.1 512.8 %all-reduce.9.cloned.1.call-start = ((), (), s32[]{:S(2)}) async-start(), calls=%async_computation.7 | async-start | bytes 172032 | tf_op jit(solution)/shard_map/psum | solution.py:254
  290.8 1.1 copy-start.9
  292.0 62.3 %copy-start.16 = (bf16[384,1152]{1,0:T(8,128)(2,1)S(1)}, bf16[384,1152]{1,0:T(8,128)(2,1)}, u32[]{:S(2)}) copy-start(bf16[384,1152]{1,0:T(8,128)(2,1)} %param.26) | copy-start | bytes 2654212
  292.0 62.3 %copy-start.25 = (f32[384]{0:T(512)S(1)}, f32[384]{0:T(512)}, u32[]{:S(2)}) copy-start(f32[384]{0:T(512)} %copy-done.24) | copy-start | bytes 4612
  297.7 62.1 %copy-start.30 = (f32[384]{0:T(512)S(1)}, f32[384]{0:T(512)}, u32[]{:S(2)}) copy-start(f32[384]{0:T(512)} %copy-done.29) | copy-start | bytes 4612
  354.3 5.4 copy-start.19
  354.3 5.4 copy-start.20
  354.3 5.4 copy-start.50
  365.7 3.1 copy-start.39
  365.7 3.1 copy-start.41
  365.7 3.1 copy-start.43
  365.7 3.1 copy-start.45
  365.7 3.3 copy-start.23
  368.7 3.3 copy-start.10
  370.0 403.5 %all-gather.14.cloned.1.call-start = ((), (), s32[]{:S(2)}) async-start(), calls=%async_computation.8 | async-start | bytes 1216512 | tf_op jit(solution)/shard_map/all_gather | solution.py:243
  383.6 5.8 copy-start.31
  383.6 5.8 copy-start.33
  383.6 5.9 copy-start.32
  383.6 5.9 copy-start.34
  383.6 5.9 copy-start.35
  383.7 5.9 copy-start.36
  383.7 5.9 copy-start.37
  383.7 5.9 copy-start.26
  383.7 5.9 copy-start.27
  383.7 5.9 copy-start.28
  389.6 204.9 %copy-start.7 = (f32[8,144,384]{2,1,0:T(8,128)S(1)}, f32[8,144,384]{2,1,0:T(8,128)}, u32[]{:S(2)}) copy-start(f32[8,144,384]{2,1,0:T(8,128)} %copy-done.6) | copy-start | bytes 5308420
  389.6 204.9 %copy-start.53 = (f32[384]{0:T(512)S(1)}, f32[384]{0:T(512)}, u32[]{:S(2)}) copy-start(f32[384]{0:T(512)} %param.32) | copy-start | bytes 4612
  591.5 185.4 %all-gather.16.cloned.1.call-start = ((), (), s32[]{:S(2)}) async-start(), calls=%async_computation.9 | async-start | bytes 1216512 | tf_op jit(solution)/shard_map/all_gather | solution.py:246
  592.9 187.1 %all-gather.12.cloned.1.call-start = ((), (), s32[]{:S(2)}) async-start(), calls=%async_computation.6 | async-start | bytes 2433024 | tf_op jit(solution)/shard_map/all_gather | solution.py:249
  768.6 1.7 copy-start.14
  776.9 8.2 %copy-start.1 = (bf16[384,1536]{1,0:T(8,128)(2,1)S(1)}, bf16[384,1536]{1,0:T(8,128)(2,1)}, u32[]{:S(2)}) copy-start(bf16[384,1536]{1,0:T(8,128)(2,1)} %param.29) | copy-start | bytes 3538948
Sparse Core Ops, SparseCore 0:
  23.9 72.6 all-gather.9
  98.7 68.5 all-gather.7
  220.4 64.9 reduce-scatter.4
  287.6 66.6 reduce-scatter.2
  370.1 122.4 all-reduce.8
  591.6 53.8 all-gather.13
  648.3 53.5 all-gather.15
  705.3 58.1 all-gather.11
where the time goes:
time: 800 us; the launch traced here: 792 us
  blocking collectives  360 us (45%)
  waiting for transfers between devices  176 us (22%)
  matrix products  116 us (14%)
  local copies, waits for them, and re-layouts  88.6 us (11%)
  other arithmetic  35.7 us (4%)
  between operations  15.4 us (2%)
    unnamed x1, blocking collectives  200 us
    all_gather x1, blocking collectives, per_device(): lax.all_gather(shares[0].astype(jnp.bfloat16), ('img', 'strip'), axis=0,...  88.5 us
    all_gather x1, blocking collectives, per_device(): lax.all_gather(shares[1].astype(jnp.bfloat16), ('img', 'strip'), axis=0,...  71 us
    all_gather x1, waiting for transfers between devices, per_device(): lax.all_gather(keys_local, 'strip', axis=1, tiled=True)  66.5 us
    reduce_scatter x1, waiting for transfers between devices, per_device(): lax.psum_scatter(g_keys_all.reshape(images, seq_all, model_width).astype(...  56.6 us
    all_gather x1, waiting for transfers between devices, per_device(): lax.all_gather(values_local, 'strip', axis=1, tiled=True)  52.9 us
  transfers between devices with their start and end apart: 8, of which 3 were waited for; matrix products, arithmetic and copies ran while one was open for 18% of the time, Pallas kernels for 0%

commit v1 on v0

v1 whole, which is shorter than its diff:
```python
import functools
import math
from types import SimpleNamespace

import jax
import jax.numpy as jnp
from jax import lax
from jax.experimental import pallas as pl
from jax.experimental.pallas import tpu as pltpu
from jax.sharding import PartitionSpec as P

HD = 64
EPSILON = 1e-06
MESH = pl.DeviceIdType.MESH
HIGHEST = lax.Precision.HIGHEST
BF = jnp.bfloat16
F32 = jnp.float32
COMM = True
MAIN, TAIL, COT = 0, 1, 2
IMG, STRIP = "img", "strip"
REP = {}


def begin(copy):
    copy.start()


def landed(copy):
    copy.wait_recv()


def sent(copy):
    copy.wait_send()


def nn(a, b, precision=None):
    return lax.dot_general(
        a, b, (((1,), (0,)), ((), ())), precision=precision, preferred_element_type=F32
    )


def nt(a, b):
    return lax.dot_general(a, b, (((1,), (1,)), ((), ())), preferred_element_type=F32)


def tn(a, b, precision=None):
    return lax.dot_general(
        a, b, (((0,), (0,)), ((), ())), precision=precision, preferred_element_type=F32
    )


def fold8(x):
    return jnp.sum(x.reshape(x.shape[0] // 8, 8, x.shape[1]), axis=0)


def rows_of(start, size):
    return pl.ds(pl.multiple_of(start, 16), size)


def chunk_of(rows):
    best = 16
    for size in range(16, 257, 16):
        if rows % size == 0:
            best = size
    return best


class Reduce:
    def __init__(self, rows, stages, extra, grad, out, recv, extra_recv, sems):
        self.rows, self.stages, self.extra, self.done = rows, stages, extra, 0
        self.grad, self.out, self.recv, self.extra_recv = grad, out, recv, extra_recv
        self.rs_s, self.rs_r, self.ag_s, self.ag_r, self.ex_s, self.ex_r, self.loc = sems
        sizes, offsets = [rows], [0]
        for axis, unit, size in stages:
            mine = self.index(axis, unit, size)
            sizes.append(sizes[-1] // size)
            offsets.append(offsets[-1] + mine * sizes[-1])
        self.sizes, self.offsets = sizes, offsets

    @staticmethod
    def index(axis, unit, size):
        return (lax.axis_index(axis) // unit) % size

    def peer(self, stage, d):
        axis, unit, size = stage
        mine = self.index(axis, unit, size)
        there = (mine + d) % size
        return {axis: lax.axis_index(axis) + unit * (there - mine)}, there

    def rs_copies(self, k):
        size, sub = self.stages[k][2], self.sizes[k + 1]
        copies = []
        for d in range(1, size):
            device, there = self.peer(self.stages[k], d)
            copies.append(
                pltpu.make_async_remote_copy(
                    src_ref=self.grad.at[rows_of(self.offsets[k] + there * sub, sub), :],
                    dst_ref=self.recv[k].at[d - 1],
                    send_sem=self.rs_s.at[k, d - 1],
                    recv_sem=self.rs_r.at[k, d - 1],
                    device_id=device,
                    device_id_type=MESH,
                )
            )
        return copies

    def rs_start(self, k):
        for copy in self.rs_copies(k):
            copy.start()

    def rs_finish(self, k):
        copies = self.rs_copies(k)
        for copy in copies:
            copy.wait_recv()
        size, sub, first = self.stages[k][2], self.sizes[k + 1], self.offsets[k + 1]
        step = chunk_of(sub)

        def body(b, carry):
            rows = rows_of(first + b * step, step)
            total = self.grad[rows, :].astype(F32)
            for d in range(size - 1):
                total = total + self.recv[k][d, rows_of(b * step, step), :].astype(F32)
            self.grad[rows, :] = total.astype(BF)
            return carry

        lax.fori_loop(0, sub // step, body, 0)
        for copy in copies:
            copy.wait_send()

    def piece(self):
        return self.grad.at[rows_of(self.offsets[-1], self.sizes[-1]), :]

    def extra_copies(self):
        copies = []
        for d in range(1, self.extra[2]):
            device, _ = self.peer(self.extra, d)
            copies.append(
                pltpu.make_async_remote_copy(
                    src_ref=self.piece(),
                    dst_ref=self.extra_recv.at[d - 1],
                    send_sem=self.ex_s.at[d - 1],
                    recv_sem=self.ex_r.at[d - 1],
                    device_id=device,
                    device_id_type=MESH,
                )
            )
        return copies

    def extra_all(self):
        if self.extra is None:
            return
        copies = self.extra_copies()
        for copy in copies:
            copy.start()
        for copy in copies:
            copy.wait()
        rows = rows_of(self.offsets[-1], self.sizes[-1])
        total = self.grad[rows, :].astype(F32)
        for d in range(self.extra[2] - 1):
            total = total + self.extra_recv[d].astype(F32)
        self.grad[rows, :] = total.astype(BF)

    def ag_copies(self, k):
        size, sub = self.stages[k][2], self.sizes[k + 1]
        region = self.out.at[rows_of(self.offsets[k + 1], sub), :]
        source = self.piece() if k == len(self.stages) - 1 else region
        copies = []
        for d in range(1, size):
            device, _ = self.peer(self.stages[k], d)
            copies.append(
                pltpu.make_async_remote_copy(
                    src_ref=source,
                    dst_ref=region,
                    send_sem=self.ag_s.at[k, d - 1],
                    recv_sem=self.ag_r.at[k, d - 1],
                    device_id=device,
                    device_id_type=MESH,
                )
            )
        return copies

    def local_copy(self):
        region = self.out.at[rows_of(self.offsets[-1], self.sizes[-1]), :]
        return pltpu.make_async_copy(self.piece(), region, self.loc.at[0])

    def left(self):
        return self.done < 2 * len(self.stages) + 1

    def step(self):
        last = len(self.stages) - 1
        n = self.done
        self.done += 1
        if n == 0:
            self.rs_start(0)
        elif n <= last:
            self.rs_finish(n - 1)
            self.rs_start(n)
        elif n == last + 1:
            self.rs_finish(last)
            self.extra_all()
            self.ag_start(last)
        else:
            k = 2 * last + 2 - n
            self.ag_finish(k)
            if k > 0:
                self.ag_start(k - 1)

    def ag_start(self, k):
        if k == len(self.stages) - 1:
            self.local_copy().start()
        for copy in self.ag_copies(k):
            copy.start()

    def ag_finish(self, k):
        if k == len(self.stages) - 1:
            self.local_copy().wait()
        for copy in self.ag_copies(k):
            copy.wait()


def layer_kernel(cfg, *refs):
    r = SimpleNamespace(**dict(zip(cfg.names, refs)))
    n_strip, strip_rows, slots = cfg.n_strip, cfg.strip_rows, cfg.slots
    seq, width, ff, pixels, area = cfg.seq, cfg.width, cfg.ff, cfg.pixels, cfg.area
    main_w = cfg.main_w
    tail = pixels - main_w
    grid_side, base_count = cfg.grid_side, cfg.base_count
    pairs = width // 128
    depth = r.base_embed.shape[1]
    ff_chunks = ff // width
    me = lax.axis_index(STRIP)
    group = 2 if n_strip % 2 == 0 else 1
    block = group * strip_rows
    blocks = n_strip // group

    def repeat(fn, *args):
        count = REP.get(fn.__name__, 1)
        if count == 1:
            fn(*args)
        else:
            lax.fori_loop(0, count, lambda t, c: (fn(*args), c)[1], 0)

    stages, extra = cfg.stages, cfg.extra
    groups, at = [], len(refs) - sum(len(g.stages) + 8 for g in cfg.groups)
    for g, grad, out in zip(cfg.groups, (r.gd, r.gu, r.gq, r.gk), (r.gd_out, r.gu_out, r.gq_out, r.gk_out)):
        n = len(g.stages)
        groups.append(Reduce(g.rows, g.stages, extra, grad, out, refs[at:at + n], refs[at + n],
                             refs[at + n + 1:at + n + 8]))
        at += n + 8
    sum_d, sum_u, sum_q, sum_k = groups
    if COMM:
        barrier = pltpu.get_barrier_semaphore()
        greeted = 0
        for stage in stages + ([extra] if extra else []):
            for d in range(1, stage[2]):
                device, _ = sum_k.peer(stage, d)
                pl.semaphore_signal(barrier, inc=1, device_id=device, device_id_type=MESH)
                greeted += 1

    loads = [
        pltpu.make_async_copy(r.w_qkv, r.wqkv, r.load_sem.at[0]),
        pltpu.make_async_copy(r.w_out, r.wout, r.load_sem.at[1]),
        pltpu.make_async_copy(r.w_up, r.wup, r.load_sem.at[2]),
        pltpu.make_async_copy(r.w_down, r.wdown, r.load_sem.at[3]),
    ]
    base_loads = [
        pltpu.make_async_copy(r.base_embed.at[c], r.wide.at[rows_of(c * depth, depth), :], r.load_sem.at[4 + c])
        for c in range(3)
    ]
    tails_load = pltpu.make_async_copy(
        r.patches.at[:, :, main_w:pixels], r.ptails, r.load_sem.at[7]
    )
    own_loads = []
    for slot in range(slots):
        rows = rows_of(me * strip_rows, strip_rows)
        own_loads.append(pltpu.make_async_copy(
            r.patches.at[me * slots + slot, :, 0:main_w], r.pmain.at[slot, rows, :],
            r.load_sem.at[8 + slot]))
        own_loads.append(pltpu.make_async_copy(
            r.cotangent.at[me * slots + slot], r.cot.at[slot, rows, :],
            r.load_sem.at[8 + slots + slot]))
    tails_load.start()
    for copy in base_loads:
        copy.start()
    for copy in own_loads:
        copy.start()
    for copy in loads:
        copy.start()

    def z_in(kind, slot, d):
        home = (me + d) % n_strip
        rows = rows_of(me * strip_rows, strip_rows)
        image = home * slots + slot
        if kind == MAIN:
            src, dst, k = r.patches.at[image, :, 0:main_w], r.pmain.at[slot, rows, :], slot
        elif kind == TAIL:
            src, dst, k = r.packed.at[home], r.ptail.at[rows, :], slots
        else:
            src, dst, k = r.cotangent.at[image], r.cot.at[slot, rows, :], slots + 1 + slot
        return pltpu.make_async_remote_copy(
            src_ref=src, dst_ref=dst, send_sem=r.zin_s.at[k, d - 1],
            recv_sem=r.zin_r.at[k, d - 1], device_id={STRIP: home}, device_id_type=MESH)

    def z_all(kind, slot, act):
        if not COMM:
            return
        for d in range(1, n_strip):
            act(z_in(kind, slot, d))

    if COMM:
        pl.semaphore_wait(barrier, greeted)
    z_all(MAIN, 0, begin)

    tails_load.wait()
    zero_tail = jnp.zeros((strip_rows, 128 // slots - tail), F32)
    for home in range(n_strip):
        parts = []
        for slot in range(slots):
            parts.append(r.ptails[home * slots + slot].astype(F32))
            parts.append(zero_tail)
        r.packed[home] = jnp.concatenate(parts, axis=1).astype(BF)
    z_all(TAIL, 0, begin)
    for slot in range(1, slots):
        z_all(MAIN, slot, begin)
    r.ptail[rows_of(me * strip_rows, strip_rows), :] = r.packed[me]

    def make_kernel():
        pinv = r.pinv[...].astype(BF)
        r.kf[...] = jnp.zeros_like(r.kf)
        for c in range(3):
            if not REP:
                base_loads[c].wait()
            r.kf[c * area:(c + 1) * area, :] = nn(pinv, r.wide[c * depth:(c + 1) * depth, :].astype(BF))
        kernel = r.kf[...].astype(BF)
        r.kmain[...] = kernel[0:main_w]
        for slot in range(slots):
            r.stage[...] = jnp.zeros_like(r.stage)
            at = slot * (128 // slots)
            r.stage[at:at + tail, :] = r.kf[main_w:pixels, :]
            r.ktail[slot] = r.stage[...].astype(BF)

    if REP:
        for copy in base_loads:
            copy.wait()
    repeat(make_kernel)

    def make_position():
        cells = r.table.shape[0]
        cell = lax.broadcasted_iota(jnp.int32, (cells, grid_side), 0).astype(F32)
        grid_row = jnp.floor((cell + 0.5) / base_count)
        corner = (grid_row, cell - grid_row * base_count)
        place = lax.broadcasted_iota(jnp.int32, (grid_side, seq), 1).astype(F32)
        which = lax.broadcasted_iota(jnp.int32, (grid_side, seq), 0).astype(F32)
        patch_row = jnp.floor((place + 0.5) / grid_side)
        patch = (patch_row, place - patch_row * grid_side)
        product = None
        for t in range(2):
            low = r.pos_index[t, 0:1, :].astype(F32)
            high = r.pos_index[t, 1:2, :].astype(F32)
            frac = r.pos_frac[t:t + 1, :]
            entry = (1.0 - frac) * (corner[t] == low).astype(F32) + frac * (corner[t] == high).astype(F32)
            spread = nn(entry, (patch[t] == which).astype(F32), HIGHEST)
            product = spread if product is None else product * spread
        valid = lax.broadcasted_iota(jnp.int32, (cells, seq), 0) < base_count * base_count
        r.table[...] = jnp.where(valid, product, 0.0)
        r.stage[...] = jnp.zeros_like(r.stage)
        for b in range(base_count):
            r.stage[b * base_count:(b + 1) * base_count, :] = r.pos_grid[b]
        r.posb[...] = tn(r.table[...], r.stage[0:cells, :], HIGHEST) + r.bias_embed[...]

    repeat(make_position)
    z_all(COT, 0, begin)
    r.sums[...] = jnp.zeros_like(r.sums)
    r.sums_up[...] = jnp.zeros_like(r.sums_up)
    for copy in loads:
        copy.wait()
    for copy in own_loads:
        copy.wait()

    def wide_rows(k, rows):
        return rows_of(k * seq + rows.start, rows.size)

    lane = lax.broadcasted_iota(jnp.int32, (1, 128), 1)
    first_head = lane < HD

    def norm(x, gain, shift):
        center = x - jnp.mean(x, axis=-1, keepdims=True)
        inv = lax.rsqrt(jnp.mean(center * center, axis=-1, keepdims=True) + EPSILON)
        unit = center * inv
        return unit * gain + shift, unit, inv

    def norm_back(g, unit, inv, gain):
        gu = g * gain
        return inv * (
            gu - jnp.mean(gu, axis=-1, keepdims=True)
            - unit * jnp.mean(gu * unit, axis=-1, keepdims=True)
        )

    def add_sum(row, x):
        r.sums[row] += fold8(x)

    B_EMBED, GAIN, SHIFT, B_Q, B_V, B_O, B_DOWN = 0, 1, 3, 5, 6, 7, 8

    def near_first(t):
        return (t + me // group) % blocks

    def wait_rows(t, kind, slot):
        if not COMM:
            return
        for part in range(group):
            d = (me - t * group - part + n_strip) % n_strip

            @pl.when(d > 0)
            def _():
                z_in(kind, slot, d).wait_recv()

    def embed(i):
        def body(b, carry):
            b = near_first(b)
            rows = rows_of(b * block, block)
            wait_rows(b, MAIN, i)
            if i == 0:
                wait_rows(b, TAIL, 0)
            emb = (
                nn(r.pmain[i, rows, :], r.kmain[...])
                + nn(r.ptail[rows, :], r.ktail[i])
                + r.posb[rows, :]
            )
            r.wide[wide_rows(i, rows), :] = emb
            y, unit, inv = norm(emb, r.norm_gain[0:1, :], r.norm_shift[0:1, :])
            y = y.astype(BF)
            r.normed[i, rows, :] = y
            r.unit[i, rows, :] = unit.astype(BF)
            r.inv[i, rows, :] = jnp.broadcast_to(inv, (block, 128))
            q = nn(y, r.wqkv[:, 0:width]) + r.bias_attn[0:1, :]
            r.qkv[i, rows, 0:width] = (q * (1.0 / math.sqrt(HD))).astype(BF)
            r.qkv[i, rows, width:2 * width] = nn(y, r.wqkv[:, width:2 * width]).astype(BF)
            v = nn(y, r.wqkv[:, 2 * width:3 * width]) + r.bias_attn[1:2, :]
            r.qkv[i, rows, 2 * width:3 * width] = v.astype(BF)
            return carry

        lax.fori_loop(0, blocks, body, 0)

    def lanes(p, part=0):
        return slice(part * width + p * 128, part * width + (p + 1) * 128)

    def ahead(tasks, front, rest, depth):
        ready = [front(*task) for task in tasks[:depth]]
        for n, task in enumerate(tasks):
            if n + depth < len(tasks):
                ready.append(front(*tasks[n + depth]))
            rest(*task, ready[n])
            ready[n] = None

    heads = [(p, h) for p in range(pairs) for h in range(2)]

    def pick(x, h):
        return jnp.where(first_head == (h == 0), x, jnp.zeros_like(x))

    def attend(i):
        outs, recips = {}, {}

        def front(p, h):
            return nt(pick(r.qkv[i, :, lanes(p)], h), r.qkv[i, :, lanes(p, 1)])

        def rest(p, h, s):
            e = jnp.exp(s - jnp.max(s, axis=-1, keepdims=True))
            recip = 1.0 / jnp.sum(e, axis=-1, keepdims=True)
            e = e.astype(BF)
            r.expo[i, 2 * p + h] = e
            outs[h] = nn(e, r.qkv[i, :, lanes(p, 2)]) * recip
            recips[h] = jnp.broadcast_to(recip, (seq, 128))
            if h == 1:
                r.att[i, :, lanes(p)] = jnp.where(first_head, outs[0], outs[1]).astype(BF)
                r.wide[(2 * slots + i) * seq:(2 * slots + i + 1) * seq, lanes(p)] = jnp.where(first_head, recips[0], recips[1])

        ahead(heads, front, rest, 2)

    c0 = math.sqrt(2.0 / math.pi)
    c1 = 0.044715

    def send_rows(t, i, remote, own):
        if not COMM:
            return
        for part in range(group):
            strip = t * group + part
            d = (strip - me + n_strip) % n_strip

            @pl.when(d > 0)
            def _():
                remote(i, d).start()

            @pl.when(d == 0)
            def _():
                own(i).start()

    def out_copy(i, d):
        strip = (me + d) % n_strip
        return pltpu.make_async_remote_copy(
            src_ref=r.outb.at[i, rows_of(strip * strip_rows, strip_rows), :],
            dst_ref=r.output.at[me * slots + i],
            send_sem=r.zout_s.at[i, d - 1], recv_sem=r.zout_r.at[i, d - 1],
            device_id={STRIP: strip}, device_id_type=MESH)

    def own_out(i):
        return pltpu.make_async_copy(
            r.outb.at[i, rows_of(me * strip_rows, strip_rows), :],
            r.output.at[me * slots + i], r.own_sem.at[i])

    def mlp(i):
        def body(t, carry):
            t = near_first(t)
            rows = rows_of(t * block, block)
            wait_rows(t, COT, i)
            mid = r.wide[wide_rows(i, rows), :] + nn(r.att[i, rows, :], r.wout[...]) + r.bias_attn[2:3, :]
            gain = r.norm_gain[1:2, :]
            y, unit, inv = norm(mid, gain, r.norm_shift[1:2, :])
            y = y.astype(BF)
            r.nm[i, rows, :] = y
            cot = r.cot[i, rows, :]

            def front(cols):
                return nn(y, r.wup[:, cols]), nt(cot, r.wdown[cols, :])

            def rest(cols, ready):
                u = ready[0] + r.bias_up[cols]
                square = u * u
                half = 0.5 + 0.5 * jnp.tanh(u * (c0 + (c0 * c1) * square))
                act = u * half
                r.act[i, rows, cols] = act.astype(BF)
                slope = half + (act - act * half) * (2.0 * c0 + (6.0 * c0 * c1) * square)
                gu = ready[1] * slope
                r.gup[i, rows, cols] = gu.astype(BF)
                r.sums_up[:, cols] += fold8(gu)

            ahead([(slice(c, c + 256),) for c in range(0, ff, 256)], front, rest, 1)
            out = mid + r.bias_down[...] + nn(r.act[i, rows, :], r.wdown[...])
            g_nm = nt(r.gup[i, rows, :], r.wup[...])
            r.outb[i, rows, :] = out.astype(BF)
            send_rows(t, i, out_copy, own_out)
            add_sum(GAIN + 1, g_nm * unit)
            add_sum(SHIFT + 1, g_nm)
            cotf = cot.astype(F32)
            add_sum(B_DOWN, cotf)
            g_mid = cotf + norm_back(g_nm, unit, inv, gain)
            r.wide[wide_rows(slots + i, rows), :] = g_mid
            add_sum(B_O, g_mid)
            gb = g_mid.astype(BF)
            r.gb[i, rows, :] = gb
            r.datt[i, rows, :] = (nt(gb, r.wout[...]) * r.wide[wide_rows(2 * slots + i, rows), :]).astype(BF)
            return carry

        lax.fori_loop(0, blocks, body, 0)

    def ds_slot(p, h):
        wide = -(-seq // 128) * 128
        return (r.act, r.gup)[p % 2].at[slots - 1, :, h * wide:h * wide + seq]

    def attend_back(i):
        gq = {}

        def front(p, h):
            return nt(pick(r.datt[i, :, lanes(p)], h), r.qkv[i, :, lanes(p, 2)])

        def rest(p, h, dp):
            prod = r.datt[i, :, lanes(p)].astype(F32) * r.att[i, :, lanes(p)].astype(F32)
            delta = jnp.sum(pick(prod, h), axis=-1, keepdims=True)
            expo = r.expo[i, 2 * p + h]
            ds = (expo.astype(F32) * (dp - delta)).astype(BF)
            ds_slot(p, h)[...] = ds
            gq[h] = nn(ds, r.qkv[i, :, lanes(p, 1)])
            if h == 0:
                return
            g_q = jnp.where(first_head, gq[0], gq[1]) * (1.0 / math.sqrt(HD))
            r.gproj[i, :, lanes(p)] = g_q.astype(BF)
            q_t, d_t = r.qkv[i, :, lanes(p)].T, r.datt[i, :, lanes(p)].T
            for part in range(2):
                half = slice(part * HD, (part + 1) * HD)
                r.tk[p, half, :] = nn(q_t[half, :], ds_slot(p, part)[...]).astype(BF)
                r.tv[p, half, :] = nn(d_t[half, :], r.expo[i, 2 * p + part]).astype(BF)
            r.gproj[i, :, lanes(p, 1)] = r.tk[p].T
            r.gproj[i, :, lanes(p, 2)] = r.tv[p].T

        ahead(heads, front, rest, 1)

    def gp_copy(i, d):
        strip = (me + d) % n_strip
        return pltpu.make_async_remote_copy(
            src_ref=r.gup.at[i, rows_of(strip * strip_rows, strip_rows), ff - main_w:ff],
            dst_ref=r.gp_main.at[me * slots + i],
            send_sem=r.zout_s.at[slots + i, d - 1], recv_sem=r.zout_r.at[slots + i, d - 1],
            device_id={STRIP: strip}, device_id_type=MESH)

    def own_gp(i):
        return pltpu.make_async_copy(
            r.gup.at[i, rows_of(me * strip_rows, strip_rows), ff - main_w:ff],
            r.gp_main.at[me * slots + i], r.own_sem.at[slots + i])

    def gpt_copy(i, d):
        strip = (me + d) % n_strip
        return pltpu.make_async_remote_copy(
            src_ref=r.gpt.at[rows_of(strip * strip_rows, strip_rows), :],
            dst_ref=r.gp_tail.at[me],
            send_sem=r.zout_s.at[2 * slots, d - 1], recv_sem=r.zout_r.at[2 * slots, d - 1],
            device_id={STRIP: strip}, device_id_type=MESH)

    def own_gpt(i):
        return pltpu.make_async_copy(
            r.gpt.at[rows_of(me * strip_rows, strip_rows), :],
            r.gp_tail.at[me], r.own_sem.at[2 * slots])

    def embed_back(i):
        def body(t, carry):
            rows = rows_of(t * block, block)
            gain = r.norm_gain[0:1, :]
            unit = r.unit[i, rows, :].astype(F32)
            gproj = r.gproj[i, rows, :]
            add_sum(B_Q, gproj[:, 0:width].astype(F32))
            add_sum(B_V, gproj[:, 2 * width:3 * width].astype(F32))
            g_n = nt(gproj, r.wqkv[...])
            add_sum(GAIN, g_n * unit)
            add_sum(SHIFT, g_n)
            inv = r.inv[i, rows, :][:, 0:1]
            g_emb = r.wide[wide_rows(slots + i, rows), :] + norm_back(g_n, unit, inv, gain)
            add_sum(B_EMBED, g_emb)
            ge = g_emb.astype(BF)
            r.act[i, rows, ff - width:ff] = ge
            r.gup[i, rows, ff - main_w:ff] = nt(ge, r.kmain[...]).astype(BF)
            part = nt(ge, r.ktail[i])
            if i > 0:
                part = part + r.gpt[rows, :].astype(F32)
            r.gpt[rows, :] = part.astype(BF)
            send_rows(t, i, gp_copy, own_gp)
            if i == slots - 1:
                send_rows(t, i, gpt_copy, own_gpt)
            return carry

        lax.fori_loop(0, blocks, body, 0)

    def both(ref, cols=slice(None)):
        return ref[:, :, cols].reshape(slots * seq, -1)

    def grads_d():
        lhs = both(r.cot).T
        for c in range(0, ff, 512):
            r.gd[c:c + 512, :] = nn(lhs, both(r.act, slice(c, c + 512))).T.astype(BF)

    def grads_u():
        lhs = both(r.nm).T
        for c in range(0, ff, 512):
            part = nn(lhs, both(r.gup, slice(c, c + 512))).astype(BF)
            for n in range(4):
                r.gu[(c // 128 + n) * width:(c // 128 + n + 1) * width, :] = part[:, n * 128:(n + 1) * 128]

    def grads_q():
        part = tn(both(r.att), both(r.gb)).astype(BF)
        for n in range(pairs):
            r.gq[(3 * pairs + n) * width:(3 * pairs + n + 1) * width, :] = part[:, n * 128:(n + 1) * 128]
        lhs = both(r.normed).T
        for c in range(3):
            part = nn(lhs, both(r.gproj, slice(c * width, (c + 1) * width))).astype(BF)
            for n in range(pairs):
                at = (c * pairs + n) * width
                r.gq[at:at + width, :] = part[:, n * 128:(n + 1) * 128]

    def grads_k():
        r.kf[0:main_w, :] = tn(both(r.pmain), both(r.act, slice(ff - width, ff)))
        at = main_w
        total = None
        for slot in range(slots):
            part = tn(r.ptail[...], r.act[slot, :, ff - width:ff])
            start = slot * (128 // slots)
            part = part[start:start + tail, :]
            total = part if total is None else total + part
        r.kf[main_w:pixels, :] = total
        summed = sum(r.act[slot, :, ff - width:ff].astype(F32) for slot in range(slots))
        g_grid = nn(r.table[...], summed, HIGHEST)
        cells = base_count * base_count
        r.kf[pixels:pixels + cells, :] = g_grid[0:cells, :]
        small = jnp.sum(r.sums[...], axis=1)
        at = cfg.small_at + small.shape[0]
        r.kf[cfg.small_at:at, :] = small
        small_up = jnp.sum(r.sums_up[...], axis=0, keepdims=True)
        for c in range(ff_chunks):
            r.kf[at + c:at + c + 1, :] = small_up[:, c * width:(c + 1) * width]
        r.gk[0:r.kf.shape[0], :] = r.kf[...].astype(BF)
        if cfg.groups[3].rows > r.kf.shape[0]:
            more = cfg.groups[3].rows - r.kf.shape[0]
            r.gk[r.kf.shape[0]:, :] = jnp.zeros((more, width), BF)

    def step(*sums):
        if COMM:
            for one in sums:
                if one.left():
                    one.step()

    for i in range(slots):
        repeat(embed, i)
        if i + 1 < slots:
            z_all(COT, i + 1, begin)
        repeat(attend, i)
    for i in range(slots):
        repeat(mlp, i)
        if i < slots - 1:
            repeat(attend_back, i)
    repeat(grads_d)
    step(sum_d)
    repeat(grads_u)
    step(sum_u, sum_d)
    for i in range(slots - 1):
        repeat(embed_back, i)
    step(sum_u)
    repeat(attend_back, slots - 1)
    repeat(grads_q)
    step(sum_q, sum_d)
    repeat(embed_back, slots - 1)
    step(sum_q, sum_u)
    repeat(grads_k)
    step(sum_k, sum_d, sum_k, sum_u, sum_d, sum_q, sum_k, sum_u, sum_q, sum_k, sum_d, sum_q, sum_k, sum_u)
    while COMM and any(one.left() for one in groups):
        step(sum_d, sum_q, sum_k, sum_u)
    if COMM:
        for slot in range(slots):
            z_all(MAIN, slot, sent)
            z_all(COT, slot, sent)
            for d in range(1, n_strip):
                out_copy(slot, d).wait()
                gp_copy(slot, d).wait()
            own_out(slot).wait()
            own_gp(slot).wait()
        z_all(TAIL, 0, sent)
        for d in range(1, n_strip):
            gpt_copy(0, d).wait()
        own_gpt(0).wait()


def finish_kernel(cfg, *refs):
    r = SimpleNamespace(**dict(zip(cfg.names, refs)))
    width, ff, slots = cfg.width, cfg.ff, cfg.slots
    pixels, area, main_w = cfg.pixels, cfg.area, cfg.main_w
    tail = pixels - main_w
    ff_chunks = ff // width
    copies = []

    def load(k, src, dst):
        copy = pltpu.make_async_copy(src, dst, r.sem.at[k])
        copy.start()
        return copy

    def send(src, dst, k):
        copy = pltpu.make_async_copy(src, dst, r.sem.at[k])
        copy.start()
        copies.append(copy)

    loads = [
        load(9, r.gk.at[0:r.kf.shape[0], :], r.tail_in),
        load(10, r.gd, r.gd_in),
        load(11, r.gu, r.gu_in),
        load(12, r.gp_main, r.main_in),
        load(13, r.gp_tail, r.last_in),
        load(14, r.out_in, r.out_buf),
        load(15, r.gq, r.gq_in),
    ]
    loads[0].wait()
    r.kf[...] = r.tail_in[...].astype(F32)
    pinv = r.pinv[...].astype(BF)
    for c in range(3):
        part = r.kf[c * area:(c + 1) * area, :].astype(BF)
        r.base[c] = tn(pinv, part)
        send(r.base.at[c], r.g_base.at[c], 1 + c)
    loads[1].wait()
    r.down[...] = r.gd_in[...].astype(F32)
    send(r.down, r.g_down, 4)
    loads[2].wait()
    for n in range(ff // 128):
        r.up[:, n * 128:(n + 1) * 128] = r.gu_in[n * width:(n + 1) * width, :].astype(F32)
    send(r.up, r.g_up, 5)
    loads[6].wait()
    pairs = width // 128
    for n in range(3 * pairs):
        r.qkv[:, n * 128:(n + 1) * 128] = r.gq_in[n * width:(n + 1) * width, :].astype(F32)
    send(r.qkv, r.g_qkv, 6)
    for n in range(pairs):
        at = (3 * pairs + n) * width
        r.wo[:, n * 128:(n + 1) * 128] = r.gq_in[at:at + width, :].astype(F32)
    send(r.wo, r.g_out, 7)
    loads[5].wait()
    send(r.out_buf, r.output, 0)
    loads[3].wait()
    loads[4].wait()
    for image in range(r.gp.shape[0]):
        r.gp[image, :, 0:main_w] = r.main_in[image]
        start = (image % slots) * (128 // slots)
        last = r.last_in[image // slots].astype(F32)[:, start:start + tail]
        r.gp[image, :, main_w:pixels] = last.astype(BF)
    send(r.gp, r.g_patches, 8)
    small = r.kf[cfg.small_at:cfg.small_at + 16, :]
    for b in range(cfg.base_count):
        at = pixels + b * cfg.base_count
        r.g_grid[b] = r.kf[at:at + cfg.base_count, :]
    r.g_bias_embed[...] = small[0]
    r.g_gain[...] = small[1:3]
    r.g_shift[...] = small[3:5]
    r.g_attn[...] = small[5:8]
    r.g_bias_down[...] = small[8]
    for c in range(ff_chunks):
        r.g_bias_up[c * width:(c + 1) * width] = small[9 + c]
    for copy in copies:
        copy.wait()


def per_device(cfg, patches, pinv, base_embed, bias_embed, pos_grid, pos_index, pos_frac, norm_gain,
               norm_shift, w_qkv, bias_attn, w_out, w_up, bias_up, w_down, bias_down, cotangent):
    images, strip_rows, pixels = patches.shape
    width, ff = w_up.shape
    n_img, n_strip = cfg.n_img, cfg.n_strip
    slots = images // n_strip
    seq = strip_rows * n_strip
    base_count = pos_grid.shape[0]
    area = pinv.shape[0]
    main_w = pixels // 128 * 128
    core = [(IMG, 1, min(2, n_img))]
    plane = [(IMG, 2, min(4, n_img // 2))] if n_img > 2 else []
    stages = core + plane + [(STRIP, 1, n_strip)]
    left = n_img // 8
    extra = (IMG, 8, left) if left > 1 else None
    parts = math.prod(s[2] for s in stages)
    unit = 16 * parts
    cells = base_count * base_count
    small_at = -(-(pixels + cells) // 8) * 8
    k_rows = -(-(small_at + 9 + ff // width) // 128) * 128

    def sum_of(values, lanes, order):
        return SimpleNamespace(rows=-(-(values // lanes) // unit) * unit, lanes=lanes, stages=order)

    groups = [sum_of(ff * width, width, stages), sum_of(ff * width, 128, stages),
              sum_of(4 * width * width, 128, stages), sum_of(k_rows * width, width, stages)]
    conf = SimpleNamespace(n_strip=n_strip, strip_rows=strip_rows, slots=slots, seq=seq, width=width, ff=ff,
                           pixels=pixels, area=area, main_w=main_w, grid_side=pos_frac.shape[1],
                           base_count=base_count, stages=stages, extra=extra, groups=groups,
                           small_at=small_at)
    vmem = pl.BlockSpec(memory_space=pltpu.VMEM)
    hbm = pl.BlockSpec(memory_space=pl.ANY)
    ins = dict(
        patches=(patches, hbm), cotangent=(cotangent, hbm), base_embed=(base_embed, hbm),
        w_qkv=(w_qkv, hbm), w_out=(w_out, hbm), w_up=(w_up, hbm), w_down=(w_down, hbm),
        pinv=(pinv, vmem), bias_embed=(bias_embed, vmem), pos_grid=(pos_grid, vmem),
        pos_index=(pos_index, vmem), pos_frac=(pos_frac, vmem), norm_gain=(norm_gain, vmem),
        norm_shift=(norm_shift, vmem), bias_attn=(bias_attn, vmem),
        bias_up=(bias_up, vmem), bias_down=(bias_down, vmem),
    )
    outs = dict(
        output=jax.ShapeDtypeStruct((images, strip_rows, width), BF),
        gp_main=jax.ShapeDtypeStruct((images, strip_rows, main_w), BF),
        gp_tail=jax.ShapeDtypeStruct((n_strip, strip_rows, 128), BF),
        **dict(zip(("gd_out", "gu_out", "gq_out", "gk_out"),
                   (jax.ShapeDtypeStruct((g.rows, g.lanes), BF) for g in groups))),
    )
    V = pltpu.VMEM
    DMA = pltpu.SemaphoreType.DMA
    scratch = dict(
        wqkv=V(w_qkv.shape, BF), wout=V(w_out.shape, BF), wup=V(w_up.shape, BF), wdown=V(w_down.shape, BF),
        wide=V((max(3 * base_embed.shape[1], 3 * slots * seq), width), F32),
        ptails=V((images, strip_rows, pixels - main_w), BF), packed=V((n_strip, strip_rows, 128), BF),
        pmain=V((slots, seq, main_w), BF), ptail=V((seq, 128), BF), cot=V((slots, seq, width), BF),
        kf=V((k_rows, width), F32), kmain=V((main_w, width), BF), ktail=V((slots, 128, width), BF),
        stage=V((128, width), F32), table=V((-(-cells // 8) * 8, seq), F32), posb=V((seq, width), F32),
        normed=V((slots, seq, width), BF), unit=V((slots, seq, width), BF),
        inv=V((slots, seq, 128), F32), qkv=V((slots, seq, 3 * width), BF),
        expo=V((slots, width // HD, seq, seq), BF),
        att=V((slots, seq, width), BF), nm=V((slots, seq, width), BF),
        act=V((slots, seq, ff), BF), gup=V((slots, seq, ff), BF), outb=V((slots, seq, width), BF),
        gb=V((slots, seq, width), BF), datt=V((slots, seq, width), BF),
        tk=V((width // 128, 128, seq), BF), tv=V((width // 128, 128, seq), BF),
        gproj=V((slots, seq, 3 * width), BF), gpt=V((seq, 128), BF),
        sums=V((9, 8, width), F32), sums_up=V((8, ff), F32),
        gd=V((groups[0].rows, groups[0].lanes), BF), gu=V((groups[1].rows, groups[1].lanes), BF),
        gq=V((groups[2].rows, groups[2].lanes), BF), gk=V((groups[3].rows, groups[3].lanes), BF),
    )
    reduce_scratch = []
    more = max(left - 1, 1)
    for g in groups:
        size = g.rows
        for stage in g.stages:
            size //= stage[2]
            reduce_scratch.append(V((stage[2] - 1, size, g.lanes), BF))
        reduce_scratch.append(V((more, size, g.lanes), BF))
        reduce_scratch += [DMA((len(g.stages), 3))] * 4 + [DMA((more,))] * 2 + [DMA((1,))]
    scratch.update(
        load_sem=DMA((8 + 2 * slots,)), zin_s=DMA((2 * slots + 1, n_strip - 1)),
        zin_r=DMA((2 * slots + 1, n_strip - 1)), zout_s=DMA((2 * slots + 1, n_strip - 1)),
        zout_r=DMA((2 * slots + 1, n_strip - 1)), own_sem=DMA((2 * slots + 1,)),
    )
    conf.names = list(ins) + list(outs) + list(scratch)
    results = pl.pallas_call(
        functools.partial(layer_kernel, conf),
        out_shape=list(outs.values()),
        in_specs=[spec for _, spec in ins.values()],
        out_specs=[hbm] * len(outs),
        scratch_shapes=list(scratch.values()) + reduce_scratch,
        compiler_params=pltpu.CompilerParams(
            collective_id=0 if COMM else None, has_side_effects=True, vmem_limit_bytes=60 << 20),
        name="layer",
    )(*[value for value, _ in ins.values()])
    output, gp_main, gp_tail, gd, gu, gq, gk = results

    f_ins = dict(out_in=(output, hbm), gp_main=(gp_main, hbm), gp_tail=(gp_tail, hbm),
                 gd=(gd, hbm), gu=(gu, hbm), gq=(gq, hbm), gk=(gk, hbm), pinv=(pinv, vmem))
    shape = jax.ShapeDtypeStruct
    f_outs = dict(
        output=(shape(output.shape, BF), hbm), g_patches=(shape(patches.shape, BF), hbm),
        g_base=(shape(base_embed.shape, F32), hbm), g_bias_embed=(shape((width,), F32), vmem),
        g_grid=(shape(pos_grid.shape, F32), vmem), g_gain=(shape(norm_gain.shape, F32), vmem),
        g_shift=(shape(norm_shift.shape, F32), vmem), g_qkv=(shape(w_qkv.shape, F32), hbm),
        g_attn=(shape(bias_attn.shape, F32), vmem), g_out=(shape(w_out.shape, F32), hbm),
        g_up=(shape(w_up.shape, F32), hbm), g_bias_up=(shape((ff,), F32), vmem),
        g_down=(shape(w_down.shape, F32), hbm), g_bias_down=(shape((width,), F32), vmem),
    )
    f_scratch = dict(
        kf=V((k_rows, width), F32), base=V(base_embed.shape, F32), down=V(w_down.shape, F32),
        up=V(w_up.shape, F32), qkv=V(w_qkv.shape, F32), wo=V(w_out.shape, F32), gp=V(patches.shape, BF),
        tail_in=V((k_rows, width), BF), gd_in=V(gd.shape, BF), gu_in=V(gu.shape, BF), gq_in=V(gq.shape, BF),
        main_in=V(gp_main.shape, BF), last_in=V(gp_tail.shape, BF), out_buf=V(output.shape, BF), sem=DMA((16,)),
    )
    f_conf = SimpleNamespace(**dict(vars(conf), names=list(f_ins) + list(f_outs) + list(f_scratch)))
    final = pl.pallas_call(
        functools.partial(finish_kernel, f_conf),
        out_shape=[s for s, _ in f_outs.values()],
        in_specs=[spec for _, spec in f_ins.values()],
        out_specs=[spec for _, spec in f_outs.values()],
        scratch_shapes=list(f_scratch.values()),
        compiler_params=pltpu.CompilerParams(vmem_limit_bytes=56 << 20),
        name="finish",
    )(*[value for value, _ in f_ins.values()])
    (output, g_patches, g_base, g_bias_embed, g_grid, g_gain, g_shift, g_qkv, g_attn, g_out, g_up,
     g_bias_up, g_down, g_bias_down) = final
    return (output, g_patches, g_base, g_bias_embed, g_grid, g_gain, g_shift, g_qkv, g_attn, g_out, g_up,
            g_bias_up, g_down, g_bias_down)


def solution(mesh):
    cfg = SimpleNamespace(n_img=mesh.shape[IMG], n_strip=mesh.shape[STRIP])
    split = P(IMG, STRIP, None)
    return jax.shard_map(
        functools.partial(per_device, cfg), mesh=mesh,
        in_specs=(split,) + (P(),) * 15 + (split,),
        out_specs=(split, split) + (P(),) * 12, check_vma=False,
    )
```

time: 800 us -> 122 us (0.15)
  blocking collectives: 360 us -> 0 us
  waiting for transfers between devices: 176 us -> 0 us
  Pallas kernels: 0 us -> 121 us
  matrix products: 116 us -> 0 us
  local copies, waits for them, and re-layouts: 88.6 us -> 0 us
  other arithmetic: 35.7 us -> 0 us
  between operations: 15.4 us -> 0.84 us
    unnamed x1 -> x0, blocking collectives: 200 us -> none
    all_gather x2 -> x0, blocking collectives: 159 us -> none  [the longest x1 88.5 us: per_device(): lax.all_gather(shares[0].astype(jnp.bfloat16), ('img', 'strip'), axis=0,...]
    pallas_call x0 -> x2, Pallas kernels: none -> 121 us  [the longest x1 113 us: per_device(): pl.pallas_call(functools.partial(layer_kernel, conf), out_shape=list(outs...]
    all_gather x5 -> x0, waiting for transfers between devices: 119 us -> none  [the longest x1 66.5 us: per_device(): lax.all_gather(keys_local, 'strip', axis=1, tiled=True)]
    dot_general x27 -> x0, matrix products: 116 us -> none  [the longest x1 15.2 us: per_device(): jnp.einsum('iqhe,ikhe->ihqk', g_attended4, split_heads(values_back, head_...]
    reduce_scatter x2 -> x0, waiting for transfers between devices: 56.6 us -> none  [the longest x1 56.6 us: per_device(): lax.psum_scatter(g_keys_all.reshape(images, seq_all, model_width).astype(...]
    reshape x12 -> x0, local copies, waits for them, and re-layouts: 31.9 us -> none  [the longest x1 5.76 us: per_device(): kernel_term.reshape(-1)]
    convert_element_type x5 -> x0, local copies, waits for them, and re-layouts: 16.4 us -> none  [the longest x1 6.19 us: per_device(): g_keys_all.reshape(images, seq_all, model_width).astype(jnp.bfloat16)]
  transfers between devices with their start and end apart: 8 -> 0, of which waited for: 3 -> 0; matrix products, arithmetic and copies ran while one was open for 18% -> 0% of each run, Pallas kernels for 0% -> 0%
where the time goes in v1:
time: 122 us
  Pallas kernels  121 us (99%)
    pallas_call x1, Pallas kernels, per_device(): pl.pallas_call(functools.partial(layer_kernel, conf), out_shape=list(outs...  113 us
    pallas_call x1, Pallas kernels, per_device(): pl.pallas_call(functools.partial(finish_kernel, f_conf), out_shape=[s for...  8.02 us

profile of v1, /device:TPU:0, one launch (start us, length us, event | category | flops | bytes accessed | tf_op | source)
XLA Modules:
  0.0 121.8 jit_solution(10526336657067066576)
XLA Ops:
  0.7 112.9 %layer.1 = (bf16[8,144,384]{2,1,0:T(8,128)(2,1)}, bf16[8,144,256]{2,1,0:T(8,128)(2,1)}, bf16[4,144,128]{2,1,0:T(8,128)(2,1)}, bf16[1536,384]{1,0:T(8,128)(2,1)},...) custom-call(bf16[8,144,300]{2,1,0:T(8,128)(2,1)} %refs_0_.1, ...), custom_call_target="tpu_custom_call" | custom-call | tf_op jit(solution)/shard_map/layer/pallas_call | solution.py:895
  113.6 8.0 %finish.1 = (bf16[8,144,384]{2,1,0:T(8,128)(2,1)}, bf16[8,144,300]{2,1,0:T(8,128)(2,1)}, f32[3,1024,384]{2,1,0:T(8,128)}, f32[384]{0:T(512)}, f32[7,7,384]{2,1,0...) custom-call(bf16[8,144,384]{2,1,0:T(8,128)(2,1)} %get-tuple-element., ...), custom_call_target="tpu_custom_call" | custom-call | tf_op jit(solution)/shard_map/finish/pallas_call | solution.py:926

commit v2 on v1

--- a/solution.py
+++ b/solution.py
@@ -66,10 +66,15 @@
 
 
 class Reduce:
-    def __init__(self, rows, stages, extra, grad, out, recv, extra_recv, sems):
-        self.rows, self.stages, self.extra, self.done = rows, stages, extra, 0
+    def __init__(self, group, grad, out, recv, extra_recv, sems):
+        rows, stages = group.rows, group.stages
+        self.stages, self.extras, self.done, self.rows = stages, group.extras, 0, rows
         self.grad, self.out, self.recv, self.extra_recv = grad, out, recv, extra_recv
         self.rs_s, self.rs_r, self.ag_s, self.ag_r, self.ex_s, self.ex_r, self.loc = sems
+        count = len(stages)
+        self.phases = [(self.rs_start, self.rs_finish, k) for k in range(count)]
+        self.phases += [(self.ex_start, self.ex_finish, k) for k in range(len(self.extras))]
+        self.phases += [(self.ag_start, self.ag_finish, k) for k in range(count - 1, -1, -1)]
         sizes, offsets = [rows], [0]
         for axis, unit, size in stages:
             mine = self.index(axis, unit, size)
@@ -130,34 +135,33 @@
     def piece(self):
         return self.grad.at[rows_of(self.offsets[-1], self.sizes[-1]), :]
 
-    def extra_copies(self):
+    def ex_copies(self, k):
         copies = []
-        for d in range(1, self.extra[2]):
-            device, _ = self.peer(self.extra, d)
+        for d in range(1, self.extras[k][2]):
+            device, _ = self.peer(self.extras[k], d)
             copies.append(
                 pltpu.make_async_remote_copy(
                     src_ref=self.piece(),
-                    dst_ref=self.extra_recv.at[d - 1],
-                    send_sem=self.ex_s.at[d - 1],
-                    recv_sem=self.ex_r.at[d - 1],
+                    dst_ref=self.extra_recv[k].at[d - 1],
+                    send_sem=self.ex_s.at[k, d - 1],
+                    recv_sem=self.ex_r.at[k, d - 1],
                     device_id=device,
                     device_id_type=MESH,
                 )
             )
         return copies
 
-    def extra_all(self):
-        if self.extra is None:
-            return
-        copies = self.extra_copies()
-        for copy in copies:
+    def ex_start(self, k):
+        for copy in self.ex_copies(k):
             copy.start()
-        for copy in copies:
+
+    def ex_finish(self, k):
+        for copy in self.ex_copies(k):
             copy.wait()
         rows = rows_of(self.offsets[-1], self.sizes[-1])
         total = self.grad[rows, :].astype(F32)
-        for d in range(self.extra[2] - 1):
-            total = total + self.extra_recv[d].astype(F32)
+        for d in range(self.extras[k][2] - 1):
+            total = total + self.extra_recv[k][d].astype(F32)
         self.grad[rows, :] = total.astype(BF)
 
     def ag_copies(self, k):
@@ -184,26 +188,15 @@
         return pltpu.make_async_copy(self.piece(), region, self.loc.at[0])
 
     def left(self):
-        return self.done < 2 * len(self.stages) + 1
+        return self.done <= len(self.phases)
 
     def step(self):
-        last = len(self.stages) - 1
         n = self.done
         self.done += 1
-        if n == 0:
-            self.rs_start(0)
-        elif n <= last:
-            self.rs_finish(n - 1)
-            self.rs_start(n)
-        elif n == last + 1:
-            self.rs_finish(last)
-            self.extra_all()
-            self.ag_start(last)
-        else:
-            k = 2 * last + 2 - n
-            self.ag_finish(k)
-            if k > 0:
-                self.ag_start(k - 1)
+        if n > 0:
+            self.phases[n - 1][1](self.phases[n - 1][2])
+        if n < len(self.phases):
+            self.phases[n][0](self.phases[n][2])
 
     def ag_start(self, k):
         if k == len(self.stages) - 1:
@@ -240,18 +233,18 @@
         else:
             lax.fori_loop(0, count, lambda t, c: (fn(*args), c)[1], 0)
 
-    stages, extra = cfg.stages, cfg.extra
-    groups, at = [], len(refs) - sum(len(g.stages) + 8 for g in cfg.groups)
+    groups = []
+    at = len(refs) - sum(len(g.stages) + len(g.extras) + 7 for g in cfg.groups)
     for g, grad, out in zip(cfg.groups, (r.gd, r.gu, r.gq, r.gk), (r.gd_out, r.gu_out, r.gq_out, r.gk_out)):
-        n = len(g.stages)
-        groups.append(Reduce(g.rows, g.stages, extra, grad, out, refs[at:at + n], refs[at + n],
-                             refs[at + n + 1:at + n + 8]))
-        at += n + 8
+        n, e = len(g.stages), len(g.extras)
+        groups.append(Reduce(g, grad, out, refs[at:at + n], refs[at + n:at + n + e],
+                             refs[at + n + e:at + n + e + 7]))
+        at += n + e + 7
     sum_d, sum_u, sum_q, sum_k = groups
     if COMM:
         barrier = pltpu.get_barrier_semaphore()
         greeted = 0
-        for stage in stages + ([extra] if extra else []):
+        for stage in cfg.stages + cfg.left:
             for d in range(1, stage[2]):
                 device, _ = sum_k.peer(stage, d)
                 pl.semaphore_signal(barrier, inc=1, device_id=device, device_id_type=MESH)
@@ -320,8 +313,6 @@
             parts.append(zero_tail)
         r.packed[home] = jnp.concatenate(parts, axis=1).astype(BF)
     z_all(TAIL, 0, begin)
-    for slot in range(1, slots):
-        z_all(MAIN, slot, begin)
     r.ptail[rows_of(me * strip_rows, strip_rows), :] = r.packed[me]
 
     def make_kernel():
@@ -369,9 +360,12 @@
         r.posb[...] = tn(r.table[...], r.stage[0:cells, :], HIGHEST) + r.bias_embed[...]
 
     repeat(make_position)
-    z_all(COT, 0, begin)
     r.sums[...] = jnp.zeros_like(r.sums)
     r.sums_up[...] = jnp.zeros_like(r.sums_up)
+    for one, used in zip(groups, ((ff + width), ff * pairs, 3 * width * pairs)):
+        if one.rows > used:
+            r_pad = one.grad.shape
+            one.grad[used:, :] = jnp.zeros((r_pad[0] - used, r_pad[1]), BF)
     for copy in loads:
         copy.wait()
     for copy in own_loads:
@@ -415,12 +409,20 @@
                 z_in(kind, slot, d).wait_recv()
 
     def embed(i):
-        def body(b, carry):
-            b = near_first(b)
+        def body(t, carry):
+            b = near_first(t)
             rows = rows_of(b * block, block)
             wait_rows(b, MAIN, i)
             if i == 0:
                 wait_rows(b, TAIL, 0)
+
+            @pl.when(t == 0)
+            def _():
+                if i + 1 < slots:
+                    z_all(MAIN, i + 1, begin)
+                else:
+                    z_all(COT, i, begin)
+
             emb = (
                 nn(r.pmain[i, rows, :], r.kmain[...])
                 + nn(r.ptail[rows, :], r.ktail[i])
@@ -479,21 +481,6 @@
     c0 = math.sqrt(2.0 / math.pi)
     c1 = 0.044715
 
-    def send_rows(t, i, remote, own):
-        if not COMM:
-            return
-        for part in range(group):
-            strip = t * group + part
-            d = (strip - me + n_strip) % n_strip
-
-            @pl.when(d > 0)
-            def _():
-                remote(i, d).start()
-
-            @pl.when(d == 0)
-            def _():
-                own(i).start()
-
     def out_copy(i, d):
         strip = (me + d) % n_strip
         return pltpu.make_async_remote_copy(
@@ -507,11 +494,24 @@
             r.outb.at[i, rows_of(me * strip_rows, strip_rows), :],
             r.output.at[me * slots + i], r.own_sem.at[i])
 
+    def send_out(i):
+        if not COMM:
+            return
+        for d in range(1, n_strip):
+            out_copy(i, d).start()
+        own_out(i).start()
+
     def mlp(i):
-        def body(t, carry):
-            t = near_first(t)
+        def body(n, carry):
+            t = near_first(n)
             rows = rows_of(t * block, block)
             wait_rows(t, COT, i)
+            if i > 0:
+
+                @pl.when(n == blocks - 1)
+                def _():
+                    send_out(i - 1)
+
             mid = r.wide[wide_rows(i, rows), :] + nn(r.att[i, rows, :], r.wout[...]) + r.bias_attn[2:3, :]
             gain = r.norm_gain[1:2, :]
             y, unit, inv = norm(mid, gain, r.norm_shift[1:2, :])
@@ -537,7 +537,6 @@
             out = mid + r.bias_down[...] + nn(r.act[i, rows, :], r.wdown[...])
             g_nm = nt(r.gup[i, rows, :], r.wup[...])
             r.outb[i, rows, :] = out.astype(BF)
-            send_rows(t, i, out_copy, own_out)
             add_sum(GAIN + 1, g_nm * unit)
             add_sum(SHIFT + 1, g_nm)
             cotf = cot.astype(F32)
@@ -630,12 +629,23 @@
             if i > 0:
                 part = part + r.gpt[rows, :].astype(F32)
             r.gpt[rows, :] = part.astype(BF)
-            send_rows(t, i, gp_copy, own_gp)
-            if i == slots - 1:
-                send_rows(t, i, gpt_copy, own_gpt)
             return carry
 
         lax.fori_loop(0, blocks, body, 0)
+
+    def send_gp(i):
+        if not COMM:
+            return
+        for d in range(1, n_strip):
+            gp_copy(i, d).start()
+        own_gp(i).start()
+
+    def send_tail():
+        if not COMM:
+            return
+        for d in range(1, n_strip):
+            gpt_copy(0, d).start()
+        own_gpt(0).start()
 
     def both(ref, cols=slice(None)):
         return ref[:, :, cols].reshape(slots * seq, -1)
@@ -644,6 +654,7 @@
         lhs = both(r.cot).T
         for c in range(0, ff, 512):
             r.gd[c:c + 512, :] = nn(lhs, both(r.act, slice(c, c + 512))).T.astype(BF)
+        r.gd[ff:ff + width, :] = tn(both(r.att), both(r.gb)).astype(BF)
 
     def grads_u():
         lhs = both(r.nm).T
@@ -653,9 +664,6 @@
                 r.gu[(c // 128 + n) * width:(c // 128 + n + 1) * width, :] = part[:, n * 128:(n + 1) * 128]
 
     def grads_q():
-        part = tn(both(r.att), both(r.gb)).astype(BF)
-        for n in range(pairs):
-            r.gq[(3 * pairs + n) * width:(3 * pairs + n + 1) * width, :] = part[:, n * 128:(n + 1) * 128]
         lhs = both(r.normed).T
         for c in range(3):
             part = nn(lhs, both(r.gproj, slice(c * width, (c + 1) * width))).astype(BF)
@@ -697,26 +705,31 @@
     for i in range(slots):
         repeat(embed, i)
         if i + 1 < slots:
-            z_all(COT, i + 1, begin)
+            z_all(COT, i, begin)
         repeat(attend, i)
     for i in range(slots):
         repeat(mlp, i)
-        if i < slots - 1:
-            repeat(attend_back, i)
     repeat(grads_d)
     step(sum_d)
+    send_out(slots - 1)
     repeat(grads_u)
     step(sum_u, sum_d)
-    for i in range(slots - 1):
-        repeat(embed_back, i)
+    repeat(attend_back, 0)
     step(sum_u)
-    repeat(attend_back, slots - 1)
+    for i in range(1, slots):
+        repeat(attend_back, i)
     repeat(grads_q)
     step(sum_q, sum_d)
-    repeat(embed_back, slots - 1)
-    step(sum_q, sum_u)
+    repeat(embed_back, 0)
+    step(sum_q)
+    for i in range(1, slots):
+        repeat(embed_back, i)
     repeat(grads_k)
-    step(sum_k, sum_d, sum_k, sum_u, sum_d, sum_q, sum_k, sum_u, sum_q, sum_k, sum_d, sum_q, sum_k, sum_u)
+    step(sum_k, sum_u, sum_k, sum_d, sum_q, sum_k, sum_u, sum_d, sum_k, sum_q)
+    for i in range(slots):
+        send_gp(i)
+    send_tail()
+    step(sum_u, sum_k, sum_q, sum_d, sum_u, sum_k, sum_q, sum_d)
     while COMM and any(one.left() for one in groups):
         step(sum_d, sum_q, sum_k, sum_u)
     if COMM:
@@ -769,7 +782,9 @@
         r.base[c] = tn(pinv, part)
         send(r.base.at[c], r.g_base.at[c], 1 + c)
     loads[1].wait()
-    r.down[...] = r.gd_in[...].astype(F32)
+    r.down[...] = r.gd_in[0:ff, :].astype(F32)
+    r.wo[...] = r.gd_in[ff:ff + width, :].astype(F32)
+    send(r.wo, r.g_out, 7)
     send(r.down, r.g_down, 4)
     loads[2].wait()
     for n in range(ff // 128):
@@ -780,10 +795,6 @@
     for n in range(3 * pairs):
         r.qkv[:, n * 128:(n + 1) * 128] = r.gq_in[n * width:(n + 1) * width, :].astype(F32)
     send(r.qkv, r.g_qkv, 6)
-    for n in range(pairs):
-        at = (3 * pairs + n) * width
-        r.wo[:, n * 128:(n + 1) * 128] = r.gq_in[at:at + width, :].astype(F32)
-    send(r.wo, r.g_out, 7)
     loads[5].wait()
     send(r.out_buf, r.output, 0)
     loads[3].wait()
@@ -822,22 +833,23 @@
     core = [(IMG, 1, min(2, n_img))]
     plane = [(IMG, 2, min(4, n_img // 2))] if n_img > 2 else []
     stages = core + plane + [(STRIP, 1, n_strip)]
-    left = n_img // 8
-    extra = (IMG, 8, left) if left > 1 else None
-    parts = math.prod(s[2] for s in stages)
-    unit = 16 * parts
+    halves = [(STRIP, 1, 2), (STRIP, 2, n_strip // 2)] if n_strip % 2 == 0 else [(STRIP, 1, n_strip)]
+    left = [(IMG, 8, n_img // 8)] if n_img > 8 else []
     cells = base_count * base_count
     small_at = -(-(pixels + cells) // 8) * 8
     k_rows = -(-(small_at + 9 + ff // width) // 128) * 128
 
-    def sum_of(values, lanes, order):
-        return SimpleNamespace(rows=-(-(values // lanes) // unit) * unit, lanes=lanes, stages=order)
-
-    groups = [sum_of(ff * width, width, stages), sum_of(ff * width, 128, stages),
-              sum_of(4 * width * width, 128, stages), sum_of(k_rows * width, width, stages)]
+    def sum_of(values, lanes, order, extras):
+        unit = 16 * math.prod(s[2] for s in order)
+        return SimpleNamespace(rows=-(-(values // lanes) // unit) * unit, lanes=lanes, stages=order,
+                               extras=extras + left)
+
+    groups = [sum_of((ff + width) * width, width, stages, []), sum_of(ff * width, 128, stages, []),
+              sum_of(3 * width * width, 128, stages, []),
+              sum_of(k_rows * width, width, core + plane, halves)]
     conf = SimpleNamespace(n_strip=n_strip, strip_rows=strip_rows, slots=slots, seq=seq, width=width, ff=ff,
                            pixels=pixels, area=area, main_w=main_w, grid_side=pos_frac.shape[1],
-                           base_count=base_count, stages=stages, extra=extra, groups=groups,
+                           base_count=base_count, stages=stages, left=left, groups=groups,
                            small_at=small_at)
     vmem = pl.BlockSpec(memory_space=pltpu.VMEM)
     hbm = pl.BlockSpec(memory_space=pl.ANY)
@@ -878,14 +890,14 @@
         gq=V((groups[2].rows, groups[2].lanes), BF), gk=V((groups[3].rows, groups[3].lanes), BF),
     )
     reduce_scratch = []
-    more = max(left - 1, 1)
     for g in groups:
         size = g.rows
         for stage in g.stages:
             size //= stage[2]
             reduce_scratch.append(V((stage[2] - 1, size, g.lanes), BF))
-        reduce_scratch.append(V((more, size, g.lanes), BF))
-        reduce_scratch += [DMA((len(g.stages), 3))] * 4 + [DMA((more,))] * 2 + [DMA((1,))]
+        reduce_scratch += [V((stage[2] - 1, size, g.lanes), BF) for stage in g.extras]
+        many = max([s[2] - 1 for s in g.extras] + [1])
+        reduce_scratch += [DMA((len(g.stages), 3))] * 4 + [DMA((max(len(g.extras), 1), many))] * 2 + [DMA((1,))]
     scratch.update(
         load_sem=DMA((8 + 2 * slots,)), zin_s=DMA((2 * slots + 1, n_strip - 1)),
         zin_r=DMA((2 * slots + 1, n_strip - 1)), zout_s=DMA((2 * slots + 1, n_strip - 1)),

time: 122 us -> 117 us (0.959); the launches traced: 122 us -> 114 us
  Pallas kernels: 121 us -> 113 us
    pallas_call x1, Pallas kernels: 113 us -> 105 us  [per_device(): pl.pallas_call(functools.partial(layer_kernel, conf), out_shape=list(outs...]
where the time goes in v2:
time: 117 us; the launch traced here: 114 us
  Pallas kernels  113 us (97%)
    pallas_call x1, Pallas kernels, per_device(): pl.pallas_call(functools.partial(layer_kernel, conf), out_shape=list(outs...  105 us
    pallas_call x1, Pallas kernels, per_device(): pl.pallas_call(functools.partial(finish_kernel, f_conf), out_shape=[s for...  8.02 us

profile of v2, /device:TPU:0, one launch (start us, length us, event | category | flops | bytes accessed | tf_op | source)
XLA Modules:
  0.0 114.3 jit_solution(5096492482817555140)
XLA Ops:
  0.7 105.4 %layer.1 = (bf16[8,144,384]{2,1,0:T(8,128)(2,1)}, bf16[8,144,256]{2,1,0:T(8,128)(2,1)}, bf16[4,144,128]{2,1,0:T(8,128)(2,1)}, bf16[2048,384]{1,0:T(8,128)(2,1)},...) custom-call(bf16[8,144,300]{2,1,0:T(8,128)(2,1)} %refs_0_.1, ...), custom_call_target="tpu_custom_call" | custom-call | tf_op jit(solution)/shard_map/layer/pallas_call | solution.py:907
  106.1 8.0 %finish.1 = (bf16[8,144,384]{2,1,0:T(8,128)(2,1)}, bf16[8,144,300]{2,1,0:T(8,128)(2,1)}, f32[3,1024,384]{2,1,0:T(8,128)}, f32[384]{0:T(512)}, f32[7,7,384]{2,1,0...) custom-call(bf16[8,144,384]{2,1,0:T(8,128)(2,1)} %get-tuple-element., ...), custom_call_target="tpu_custom_call" | custom-call | tf_op jit(solution)/shard_map/finish/pallas_call | solution.py:938

commit v3 on v2

--- a/solution.py
+++ b/solution.py
@@ -74,7 +74,12 @@
         count = len(stages)
         self.phases = [(self.rs_start, self.rs_finish, k) for k in range(count)]
         self.phases += [(self.ex_start, self.ex_finish, k) for k in range(len(self.extras))]
-        self.phases += [(self.ag_start, self.ag_finish, k) for k in range(count - 1, -1, -1)]
+        for k in range(count - 1, -1, -1):
+            if group.relay and stages[k] == (IMG, 2, 4):
+                self.phases.append((self.near_start, self.near_finish, k))
+                self.phases.append((self.far_start, self.far_finish, k))
+            else:
+                self.phases.append((self.ag_start, self.ag_finish, k))
         sizes, offsets = [rows], [0]
         for axis, unit, size in stages:
             mine = self.index(axis, unit, size)
@@ -182,6 +187,43 @@
                 )
             )
         return copies
+
+    def plane(self, k):
+        mine = self.index(*self.stages[k])
+        return mine, mine + 1 - 2 * (mine % 2), mine + 2 - 4 * (mine // 2)
+
+    def plane_copy(self, k, slot, piece, part, there):
+        mine, _, _ = self.plane(k)
+        rows = self.sizes[k + 1] // (1 if part is None else 2)
+        start = self.offsets[k] + piece * self.sizes[k + 1] + (part or 0) * rows
+        region = self.out.at[rows_of(start, rows), :]
+        return pltpu.make_async_remote_copy(
+            src_ref=region, dst_ref=region, send_sem=self.ag_s.at[k, slot], recv_sem=self.ag_r.at[k, slot],
+            device_id={IMG: lax.axis_index(IMG) + 2 * (there - mine)}, device_id_type=MESH)
+
+    def near_copies(self, k):
+        mine, along_x, along_y = self.plane(k)
+        return [self.plane_copy(k, 0, mine, None, along_x), self.plane_copy(k, 1, mine, None, along_y)]
+
+    def far_copies(self, k):
+        _, along_x, along_y = self.plane(k)
+        return [self.plane_copy(k, 2, along_x, 0, along_y), self.plane_copy(k, 3, along_y, 1, along_x)]
+
+    def near_start(self, k):
+        for copy in self.near_copies(k):
+            copy.start()
+
+    def near_finish(self, k):
+        for copy in self.near_copies(k):
+            copy.wait()
+
+    def far_start(self, k):
+        for copy in self.far_copies(k):
+            copy.start()
+
+    def far_finish(self, k):
+        for copy in self.far_copies(k):
+            copy.wait()
 
     def local_copy(self):
         region = self.out.at[rows_of(self.offsets[-1], self.sizes[-1]), :]
@@ -729,19 +771,22 @@
     for i in range(slots):
         send_gp(i)
     send_tail()
-    step(sum_u, sum_k, sum_q, sum_d, sum_u, sum_k, sum_q, sum_d)
-    while COMM and any(one.left() for one in groups):
-        step(sum_d, sum_q, sum_k, sum_u)
     if COMM:
         for slot in range(slots):
             z_all(MAIN, slot, sent)
             z_all(COT, slot, sent)
             for d in range(1, n_strip):
                 out_copy(slot, d).wait()
+            own_out(slot).wait()
+        z_all(TAIL, 0, sent)
+    step(sum_u, sum_d, sum_k, sum_q, sum_u, sum_d, sum_k, sum_q, sum_u, sum_d)
+    while COMM and any(one.left() for one in groups):
+        step(sum_d, sum_q, sum_k, sum_u)
+    if COMM:
+        for slot in range(slots):
+            for d in range(1, n_strip):
                 gp_copy(slot, d).wait()
-            own_out(slot).wait()
             own_gp(slot).wait()
-        z_all(TAIL, 0, sent)
         for d in range(1, n_strip):
             gpt_copy(0, d).wait()
         own_gpt(0).wait()
@@ -773,10 +818,27 @@
         load(13, r.gp_tail, r.last_in),
         load(14, r.out_in, r.out_buf),
         load(15, r.gq, r.gq_in),
+        load(16, r.pinv, r.pinv_in),
     ]
     loads[0].wait()
     r.kf[...] = r.tail_in[...].astype(F32)
-    pinv = r.pinv[...].astype(BF)
+    small = r.kf[cfg.small_at:cfg.small_at + 16, :]
+    for b in range(cfg.base_count):
+        at = pixels + b * cfg.base_count
+        r.s_grid[b] = r.kf[at:at + cfg.base_count, :]
+    r.s_bias_embed[...] = small[0]
+    r.s_gain[...] = small[1:3]
+    r.s_shift[...] = small[3:5]
+    r.s_attn[...] = small[5:8]
+    r.s_bias_down[...] = small[8]
+    for c in range(ff_chunks):
+        r.s_bias_up[c * width:(c + 1) * width] = small[9 + c]
+    few = ((r.s_grid, r.g_grid), (r.s_bias_embed, r.g_bias_embed), (r.s_gain, r.g_gain), (r.s_shift, r.g_shift),
+           (r.s_attn, r.g_attn), (r.s_bias_down, r.g_bias_down), (r.s_bias_up, r.g_bias_up))
+    for n, (held, place) in enumerate(few):
+        send(held, place, 17 + n)
+    loads[7].wait()
+    pinv = r.pinv_in[...].astype(BF)
     for c in range(3):
         part = r.kf[c * area:(c + 1) * area, :].astype(BF)
         r.base[c] = tn(pinv, part)
@@ -805,17 +867,6 @@
         last = r.last_in[image // slots].astype(F32)[:, start:start + tail]
         r.gp[image, :, main_w:pixels] = last.astype(BF)
     send(r.gp, r.g_patches, 8)
-    small = r.kf[cfg.small_at:cfg.small_at + 16, :]
-    for b in range(cfg.base_count):
-        at = pixels + b * cfg.base_count
-        r.g_grid[b] = r.kf[at:at + cfg.base_count, :]
-    r.g_bias_embed[...] = small[0]
-    r.g_gain[...] = small[1:3]
-    r.g_shift[...] = small[3:5]
-    r.g_attn[...] = small[5:8]
-    r.g_bias_down[...] = small[8]
-    for c in range(ff_chunks):
-        r.g_bias_up[c * width:(c + 1) * width] = small[9 + c]
     for copy in copies:
         copy.wait()
 
@@ -839,12 +890,12 @@
     small_at = -(-(pixels + cells) // 8) * 8
     k_rows = -(-(small_at + 9 + ff // width) // 128) * 128
 
-    def sum_of(values, lanes, order, extras):
+    def sum_of(values, lanes, order, extras, relay=False):
         unit = 16 * math.prod(s[2] for s in order)
         return SimpleNamespace(rows=-(-(values // lanes) // unit) * unit, lanes=lanes, stages=order,
-                               extras=extras + left)
-
-    groups = [sum_of((ff + width) * width, width, stages, []), sum_of(ff * width, 128, stages, []),
+                               extras=extras + left, relay=relay)
+
+    groups = [sum_of((ff + width) * width, width, stages, [], True), sum_of(ff * width, 128, stages, [], True),
               sum_of(3 * width * width, 128, stages, []),
               sum_of(k_rows * width, width, core + plane, halves)]
     conf = SimpleNamespace(n_strip=n_strip, strip_rows=strip_rows, slots=slots, seq=seq, width=width, ff=ff,
@@ -897,7 +948,7 @@
             reduce_scratch.append(V((stage[2] - 1, size, g.lanes), BF))
         reduce_scratch += [V((stage[2] - 1, size, g.lanes), BF) for stage in g.extras]
         many = max([s[2] - 1 for s in g.extras] + [1])
-        reduce_scratch += [DMA((len(g.stages), 3))] * 4 + [DMA((max(len(g.extras), 1), many))] * 2 + [DMA((1,))]
+        reduce_scratch += [DMA((len(g.stages), 4))] * 4 + [DMA((max(len(g.extras), 1), many))] * 2 + [DMA((1,))]
     scratch.update(
         load_sem=DMA((8 + 2 * slots,)), zin_s=DMA((2 * slots + 1, n_strip - 1)),
         zin_r=DMA((2 * slots + 1, n_strip - 1)), zout_s=DMA((2 * slots + 1, n_strip - 1)),
@@ -917,22 +968,24 @@
     output, gp_main, gp_tail, gd, gu, gq, gk = results
 
     f_ins = dict(out_in=(output, hbm), gp_main=(gp_main, hbm), gp_tail=(gp_tail, hbm),
-                 gd=(gd, hbm), gu=(gu, hbm), gq=(gq, hbm), gk=(gk, hbm), pinv=(pinv, vmem))
+                 gd=(gd, hbm), gu=(gu, hbm), gq=(gq, hbm), gk=(gk, hbm), pinv=(pinv, hbm))
     shape = jax.ShapeDtypeStruct
     f_outs = dict(
         output=(shape(output.shape, BF), hbm), g_patches=(shape(patches.shape, BF), hbm),
-        g_base=(shape(base_embed.shape, F32), hbm), g_bias_embed=(shape((width,), F32), vmem),
-        g_grid=(shape(pos_grid.shape, F32), vmem), g_gain=(shape(norm_gain.shape, F32), vmem),
-        g_shift=(shape(norm_shift.shape, F32), vmem), g_qkv=(shape(w_qkv.shape, F32), hbm),
-        g_attn=(shape(bias_attn.shape, F32), vmem), g_out=(shape(w_out.shape, F32), hbm),
-        g_up=(shape(w_up.shape, F32), hbm), g_bias_up=(shape((ff,), F32), vmem),
-        g_down=(shape(w_down.shape, F32), hbm), g_bias_down=(shape((width,), F32), vmem),
+        g_base=(shape(base_embed.shape, F32), hbm), g_bias_embed=(shape((width,), F32), hbm),
+        g_grid=(shape(pos_grid.shape, F32), hbm), g_gain=(shape(norm_gain.shape, F32), hbm),
+        g_shift=(shape(norm_shift.shape, F32), hbm), g_qkv=(shape(w_qkv.shape, F32), hbm),
+        g_attn=(shape(bias_attn.shape, F32), hbm), g_out=(shape(w_out.shape, F32), hbm),
+        g_up=(shape(w_up.shape, F32), hbm), g_bias_up=(shape((ff,), F32), hbm),
+        g_down=(shape(w_down.shape, F32), hbm), g_bias_down=(shape((width,), F32), hbm),
     )
     f_scratch = dict(
         kf=V((k_rows, width), F32), base=V(base_embed.shape, F32), down=V(w_down.shape, F32),
         up=V(w_up.shape, F32), qkv=V(w_qkv.shape, F32), wo=V(w_out.shape, F32), gp=V(patches.shape, BF),
         tail_in=V((k_rows, width), BF), gd_in=V(gd.shape, BF), gu_in=V(gu.shape, BF), gq_in=V(gq.shape, BF),
-        main_in=V(gp_main.shape, BF), last_in=V(gp_tail.shape, BF), out_buf=V(output.shape, BF), sem=DMA((16,)),
+        main_in=V(gp_main.shape, BF), last_in=V(gp_tail.shape, BF), out_buf=V(output.shape, BF), pinv_in=V(pinv.shape, F32), s_grid=V(pos_grid.shape, F32), s_bias_embed=V((width,), F32),
+        s_gain=V(norm_gain.shape, F32), s_shift=V(norm_shift.shape, F32), s_attn=V(bias_attn.shape, F32),
+        s_bias_down=V((width,), F32), s_bias_up=V((ff,), F32), sem=DMA((24,)),
     )
     f_conf = SimpleNamespace(**dict(vars(conf), names=list(f_ins) + list(f_outs) + list(f_scratch)))
     final = pl.pallas_call(

time: 117 us -> 115 us (0.983); the launches traced: 114 us -> 115 us
  no operation moved by 1% of the time
where the time goes in v3:
time: 115 us
  Pallas kernels  114 us (99%)
    pallas_call x1, Pallas kernels, per_device(): pl.pallas_call(functools.partial(layer_kernel, conf), out_shape=list(outs...  106 us
    pallas_call x1, Pallas kernels, per_device(): pl.pallas_call(functools.partial(finish_kernel, f_conf), out_shape=[s for...  8.2 us

profile of v3, /device:TPU:0, one launch (start us, length us, event | category | flops | bytes accessed | tf_op | source)
XLA Modules:
  0.0 114.8 jit_solution(6151952958253305615)
XLA Ops:
  0.7 105.8 %layer.1 = (bf16[8,144,384]{2,1,0:T(8,128)(2,1)}, bf16[8,144,256]{2,1,0:T(8,128)(2,1)}, bf16[4,144,128]{2,1,0:T(8,128)(2,1)}, bf16[2048,384]{1,0:T(8,128)(2,1)},...) custom-call(bf16[8,144,300]{2,1,0:T(8,128)(2,1)} %refs_0_.1, ...), custom_call_target="tpu_custom_call" | custom-call | tf_op jit(solution)/shard_map/layer/pallas_call | solution.py:958
  106.4 8.2 %finish.1 = (bf16[8,144,384]{2,1,0:T(8,128)(2,1)}, bf16[8,144,300]{2,1,0:T(8,128)(2,1)}, f32[3,1024,384]{2,1,0:T(8,128)}, f32[384]{0:T(512)}, f32[7,7,384]{2,1,0...) custom-call(bf16[8,144,384]{2,1,0:T(8,128)(2,1)} %get-tuple-element., ...), custom_call_target="tpu_custom_call" | custom-call | tf_op jit(solution)/shard_map/finish/pallas_call | solution.py:991

commit v4 on v3

--- a/solution.py
+++ b/solution.py
@@ -339,7 +339,10 @@
     def z_all(kind, slot, act):
         if not COMM:
             return
-        for d in range(1, n_strip):
+        for k in range(n_strip - 1):
+            d = k + 1
+            if act is begin and n_strip == 4:
+                d = jnp.where(me == 2, (1, 3, 2)[k], d)
             act(z_in(kind, slot, d))
 
     if COMM:
@@ -675,11 +678,18 @@
 
         lax.fori_loop(0, blocks, body, 0)
 
+    early = 2 if n_strip > 2 else 1
+
+    def send_early():
+        if COMM:
+            gp_copy(0, early).start()
+
     def send_gp(i):
         if not COMM:
             return
         for d in range(1, n_strip):
-            gp_copy(i, d).start()
+            if i > 0 or d != early:
+                gp_copy(i, d).start()
         own_gp(i).start()
 
     def send_tail():
@@ -764,6 +774,7 @@
     step(sum_q, sum_d)
     repeat(embed_back, 0)
     step(sum_q)
+    send_early()
     for i in range(1, slots):
         repeat(embed_back, i)
     repeat(grads_k)

time: 115 us -> 113 us (0.983)
  Pallas kernels: 114 us -> 112 us
    pallas_call x1, Pallas kernels: 106 us -> 104 us  [per_device(): pl.pallas_call(functools.partial(layer_kernel, conf), out_shape=list(outs...]
where the time goes in v4:
time: 113 us
  Pallas kernels  112 us (99%)
    pallas_call x1, Pallas kernels, per_device(): pl.pallas_call(functools.partial(layer_kernel, conf), out_shape=list(outs...  104 us
    pallas_call x1, Pallas kernels, per_device(): pl.pallas_call(functools.partial(finish_kernel, f_conf), out_shape=[s for...  8.2 us

profile of v4, /device:TPU:0, one launch (start us, length us, event | category | flops | bytes accessed | tf_op | source)
XLA Modules:
  0.0 112.6 jit_solution(3195789340038532007)
XLA Ops:
  0.7 103.6 %layer.1 = (bf16[8,144,384]{2,1,0:T(8,128)(2,1)}, bf16[8,144,256]{2,1,0:T(8,128)(2,1)}, bf16[4,144,128]{2,1,0:T(8,128)(2,1)}, bf16[2048,384]{1,0:T(8,128)(2,1)},...) custom-call(bf16[8,144,300]{2,1,0:T(8,128)(2,1)} %refs_0_.1, ...), custom_call_target="tpu_custom_call" | custom-call | tf_op jit(solution)/shard_map/layer/pallas_call | solution.py:969
  104.3 8.2 %finish.1 = (bf16[8,144,384]{2,1,0:T(8,128)(2,1)}, bf16[8,144,300]{2,1,0:T(8,128)(2,1)}, f32[3,1024,384]{2,1,0:T(8,128)}, f32[384]{0:T(512)}, f32[7,7,384]{2,1,0...) custom-call(bf16[8,144,384]{2,1,0:T(8,128)(2,1)} %get-tuple-element., ...), custom_call_target="tpu_custom_call" | custom-call | tf_op jit(solution)/shard_map/finish/pallas_call | solution.py:1002

commit v5 on v4

--- a/solution.py
+++ b/solution.py
@@ -578,7 +578,7 @@
                 r.gup[i, rows, cols] = gu.astype(BF)
                 r.sums_up[:, cols] += fold8(gu)
 
-            ahead([(slice(c, c + 256),) for c in range(0, ff, 256)], front, rest, 1)
+            ahead([(slice(c, c + 256),) for c in range(0, ff, 256)], front, rest, 2)
             out = mid + r.bias_down[...] + nn(r.act[i, rows, :], r.wdown[...])
             g_nm = nt(r.gup[i, rows, :], r.wup[...])
             r.outb[i, rows, :] = out.astype(BF)

time: 113 us -> 113 us (level)
  no operation moved by 1% of the time
where the time goes in v5:
time: 113 us
  Pallas kernels  112 us (99%)
    pallas_call x1, Pallas kernels, per_device(): pl.pallas_call(functools.partial(layer_kernel, conf), out_shape=list(outs...  104 us
    pallas_call x1, Pallas kernels, per_device(): pl.pallas_call(functools.partial(finish_kernel, f_conf), out_shape=[s for...  8.2 us

profile of v5, /device:TPU:0, one launch (start us, length us, event | category | flops | bytes accessed | tf_op | source)
XLA Modules:
  0.0 112.6 jit_solution(14441238225431681831)
XLA Ops:
  0.7 103.6 %layer.1 = (bf16[8,144,384]{2,1,0:T(8,128)(2,1)}, bf16[8,144,256]{2,1,0:T(8,128)(2,1)}, bf16[4,144,128]{2,1,0:T(8,128)(2,1)}, bf16[2048,384]{1,0:T(8,128)(2,1)},...) custom-call(bf16[8,144,300]{2,1,0:T(8,128)(2,1)} %refs_0_.1, ...), custom_call_target="tpu_custom_call" | custom-call | tf_op jit(solution)/shard_map/layer/pallas_call | solution.py:969
  104.2 8.2 %finish.1 = (bf16[8,144,384]{2,1,0:T(8,128)(2,1)}, bf16[8,144,300]{2,1,0:T(8,128)(2,1)}, f32[3,1024,384]{2,1,0:T(8,128)}, f32[384]{0:T(512)}, f32[7,7,384]{2,1,0...) custom-call(bf16[8,144,384]{2,1,0:T(8,128)(2,1)} %get-tuple-element., ...), custom_call_target="tpu_custom_call" | custom-call | tf_op jit(solution)/shard_map/finish/pallas_call | solution.py:1002
